TPU v7x, 128 devices: a whole 4x4x4 slice. The times are simulated.
128 devices in a mesh: dp: 8 (over x, core), tensor: 16 (over z, y).
Axes of the slice: x: 4, y: 4, z: 4, core: 2. Of those that a mesh axis runs over, the one named last changes fastest.
Arguments:
- hidden: bfloat16 [8192, 8192], P('dp', 'tensor'), may hold values from -6 to 6
- exited: int32 [128], P('dp'), may hold values from 0 to 1, as said below
- destination: int32 [128], P('dp'), may hold values from 0 to 7, as said below
- norm_gain: float32 [8192], replicated, may hold values from 0.25 to 1.75
- query_weight: bfloat16 [8192, 8192], P('dp', 'tensor'), may hold values from -0.0625 to 0.0625
- keyvalue_weight: bfloat16 [8192, 2048], P('dp', 'tensor'), may hold values from -0.0625 to 0.0625
- output_weight: bfloat16 [8192, 8192], P('tensor', 'dp'), may hold values from -0.0625 to 0.0625
Outputs:
- updated: bfloat16 [3072, 8192], P('dp', 'tensor')
Inputs may be any that keep to these rules, and one draw needn't show every extreme that they name: In the 16 items of each data group at most 12 have exited = 0, and in some group exactly 12. `destination`: only read where exited = 0. Each data group is named by exactly 6 remaining items over all groups, and by at most 2 remaining items of one data group, a bound reached in every draw.
All inputs are finite; a program needn't handle non-finite values.
Results may differ from a plain program's by a relative error of at most 0.011.
Values may be sent and summed in bfloat16 or wider, within the bound.
A program may use at most 128 MiB of HBM per device.

v0:
```python
import jax
import jax.numpy as jnp
from jax import lax
from jax.sharding import PartitionSpec as P

HD = 128
ITEM_LEN = 64


EPSILON = 1e-05
THETA = 500000.0


def swapped(value, axis, stride):
    return lax.ppermute(value, axis, [(i, i ^ 1 << stride) for i in range(lax.axis_size(axis))])


def rotate(values, sequence_places):
    halfway = values.shape[-1] // 2
    freq_scale = THETA ** (-(jnp.arange(halfway, dtype=jnp.float32) * 2.0 / values.shape[-1]))
    rotary_phases = sequence_places[..., None] * freq_scale
    cosine = jnp.cos(rotary_phases)
    sine = jnp.sin(rotary_phases)
    first_half = values[..., :halfway]
    second_half = values[..., halfway:]
    return jnp.concatenate(
        [first_half * cosine - second_half * sine, second_half * cosine + first_half * sine],
        axis=-1,
    )


def attend(request_vectors, keys_part, values_part):
    logit_scores = jnp.einsum(
        "nlhd,nmd->nhlm", request_vectors, keys_part, preferred_element_type=jnp.float32
    )
    logit_scores = logit_scores * request_vectors.shape[-1] ** (-0.5)
    length = request_vectors.shape[1]
    causal = jnp.arange(length)[:, None] >= jnp.arange(length)[None, :]
    logit_scores = jnp.where(causal[None, None], logit_scores, -1e30)
    highest = jnp.max(logit_scores, axis=-1, keepdims=True)
    raised = jnp.exp(logit_scores - highest)
    probs = (raised / jnp.sum(raised, axis=-1, keepdims=True)).astype(jnp.bfloat16)
    return jnp.einsum(
        "nhlm,nmd->nlhd", probs, values_part, preferred_element_type=jnp.float32
    ).astype(jnp.bfloat16)


def attention_layer(block_rows, norm_gain, query_weight, keyvalue_weight, output_weight):
    row_count = block_rows.shape[0]
    gathered = lax.all_gather(block_rows, "tensor", axis=1, tiled=True)
    widened = gathered.astype(jnp.float32)
    scale_inv = lax.rsqrt(jnp.mean(widened * widened, axis=1, keepdims=True) + EPSILON)
    rescaled_hidden = (widened * scale_inv * norm_gain[None, :]).astype(jnp.bfloat16)
    query_accumulated = jnp.dot(
        rescaled_hidden,
        lax.all_gather(query_weight, "dp", axis=0, tiled=True),
        preferred_element_type=jnp.float32,
    )
    keyvalue_sum = jnp.dot(
        rescaled_hidden,
        lax.all_gather(keyvalue_weight, "dp", axis=0, tiled=True),
        preferred_element_type=jnp.float32,
    )
    sequence_places = (jnp.arange(row_count) % ITEM_LEN).astype(jnp.float32)
    head_count = query_weight.shape[1] // HD
    request_vectors = rotate(
        query_accumulated.reshape(row_count, head_count, HD), sequence_places[:, None]
    ).astype(jnp.bfloat16)
    parity = lax.axis_index("tensor") % 2
    rotated = rotate(keyvalue_sum, sequence_places).astype(jnp.bfloat16)
    own_part = jnp.where(parity == 0, rotated, keyvalue_sum.astype(jnp.bfloat16))
    partner = swapped(own_part, "tensor", 0)
    keys_part = jnp.where(parity == 0, own_part, partner)
    values_part = jnp.where(parity == 0, partner, own_part)
    item_count = row_count // ITEM_LEN
    context = attend(
        request_vectors.reshape(item_count, ITEM_LEN, head_count, HD),
        keys_part.reshape(item_count, ITEM_LEN, HD),
        values_part.reshape(item_count, ITEM_LEN, HD),
    )
    context = context.reshape(row_count, head_count * HD)
    terms = jnp.dot(
        context,
        lax.all_gather(output_weight, "dp", axis=1, tiled=True),
        preferred_element_type=jnp.float32,
    )
    summed = lax.psum_scatter(
        terms.astype(jnp.bfloat16), "tensor", scatter_dimension=1, tiled=True
    ).astype(jnp.float32)
    return (block_rows.astype(jnp.float32) + summed).astype(jnp.bfloat16)


def compact_received(received, received_flags, keep_count):
    flag_integers = received_flags.astype(jnp.int32)
    before = jnp.cumsum(flag_integers) - flag_integers
    picker = (jnp.arange(keep_count)[:, None] == before[None, :]) & (flag_integers[None, :] == 1)
    return jnp.dot(
        picker.astype(jnp.bfloat16), received, preferred_element_type=jnp.float32
    ).astype(jnp.bfloat16)


def shards(hidden, exited, destination, norm_gain, query_weight, keyvalue_weight, output_weight):
    group_number = lax.axis_size("dp")
    items_here = exited.shape[0]
    columns = hidden.shape[1]
    most_kept = 3 * items_here // 4
    taken = 3 * items_here // 8
    slot_cap = (most_kept + group_number - 1) // group_number
    capacity_sum = group_number * slot_cap
    staying = 1 - exited
    dest_onehot = (destination[:, None] == jnp.arange(group_number)[None, :]).astype(
        jnp.int32
    ) * staying[:, None]
    earlier = jnp.cumsum(dest_onehot, axis=0) - dest_onehot
    within = jnp.sum(earlier * dest_onehot, axis=1)
    slot_index = jnp.where(staying == 1, destination * slot_cap + within, -1)
    to_slot = jnp.arange(capacity_sum)[:, None] == slot_index[None, :]
    slot_flags = jnp.any(to_slot, axis=1).astype(jnp.bfloat16).reshape(group_number, slot_cap)
    item_rows = hidden.reshape(items_here, ITEM_LEN * columns)
    kept_rank = jnp.cumsum(staying) - staying
    pick_own = (jnp.arange(most_kept)[:, None] == kept_rank[None, :]) & (staying[None, :] == 1)
    local_records = jnp.dot(
        pick_own.astype(jnp.bfloat16), item_rows, preferred_element_type=jnp.float32
    ).astype(jnp.bfloat16)
    finished = attention_layer(
        local_records.reshape(most_kept * ITEM_LEN, columns),
        norm_gain,
        query_weight,
        keyvalue_weight,
        output_weight,
    )
    slot_from_kept = jnp.dot(to_slot.astype(jnp.float32), pick_own.astype(jnp.float32).T)
    outgoing = jnp.dot(
        slot_from_kept.astype(jnp.bfloat16),
        finished.reshape(most_kept, ITEM_LEN * columns),
        preferred_element_type=jnp.float32,
    ).astype(jnp.bfloat16)
    outgoing = outgoing.reshape(group_number, slot_cap, ITEM_LEN * columns)
    arrived, arrived_flags = (
        lax.all_to_all(outgoing, "dp", split_axis=0, concat_axis=0, tiled=True),
        lax.all_to_all(slot_flags, "dp", split_axis=0, concat_axis=0, tiled=True),
    )
    compact = compact_received(
        arrived.reshape(capacity_sum, ITEM_LEN * columns),
        arrived_flags.reshape(capacity_sum),
        taken,
    )
    return compact.reshape(taken * ITEM_LEN, columns)


def solution(mesh):
    placed = (
        P("dp", "tensor"),
        P("dp"),
        P("dp"),
        P(),
        P("dp", "tensor"),
        P("dp", "tensor"),
        P("tensor", "dp"),
    )
    return jax.shard_map(
        shards, mesh=mesh, in_specs=placed, out_specs=P("dp", "tensor"), check_vma=False
    )
```

profile of v0, /device:TPU:0, one launch (start us, length us, event | category | flops | bytes accessed | tf_op | source)
XLA Modules:
  0.0 387.0 jit_solution(3176905478301451299)
XLA Ops:
  8.6 0.8 fusion.18
  11.0 1.6 reshape.250
  13.0 1.4 reshape.251
  16.6 100.3 %all-gather.5.cloned.1.call-done = bf16[768,8192]{1,0:T(8,128)(2,1)} async-done(((bf16[768,512]{1,0:T(8,128)(2,1)}), bf16[768,8192]{1,0:T(8,128)(2,1)}) %all-gather.5.cloned.1.call-update) | async-done | bytes 12582928 | tf_op jit(solution)/shard_map/all_gather | solution.py:50
  116.9 7.1 %fusion.1 = f32[768]{0:T(1024)S(1)} fusion(bf16[768,8192]{1,0:T(8,128)(2,1)} %all-gather.5.cloned.1.call-done), kind=kLoop, calls=%fused_computation.6 | loop fusion | flops 18873600 | bytes 12585984 | tf_op jit(solution)/shard_map/reduce_sum | solution.py:52
  124.0 19.0 %all-gather.7.cloned.1.call-done = bf16[8192,128]{1,0:T(8,128)(2,1)} async-done(((bf16[1024,128]{1,0:T(8,128)(2,1)}), bf16[8192,128]{1,0:T(8,128)(2,1)}) %all-gather.7.cloned.1.call-update) | async-done | bytes 2097168 | tf_op jit(solution)/shard_map/all_gather | solution.py:61
  143.0 8.0 %fusion.6 = f32[768,128]{0,1:T(8,128)S(1)} fusion(bf16[8192,128]{1,0:T(8,128)(2,1)} %all-gather.7.cloned.1.call-done, bf16[768,8192]{1,0:T(8,128)(2,1)} %all-gather.5.cloned.1.call-done, f32[8192]{0:T(1024)S(1)} %copy-done.1, f32[768]{0:T(1024)S(1)} %add_rsqrt_fusion), kind=kOutput, calls=%fused_computation.11 | convolution fusion | flops 1635778560 | bytes 15109120 | tf_op jit(solution)/shard_map/dot_general | solution.py:59
  151.0 0.8 multiply_cosine_fusion
  151.9 1.7 collective-permute-start
  153.7 41.1 %all-gather.9.cloned.1.call-done = bf16[8192,512]{1,0:T(8,128)(2,1)} async-done(((bf16[1024,512]{1,0:T(8,128)(2,1)}), bf16[8192,512]{1,0:T(8,128)(2,1)}) %all-gather.9.cloned.1.call-update) | async-done | bytes 8388624 | tf_op jit(solution)/shard_map/all_gather | solution.py:56
  194.8 14.7 %fusion.4 = f32[768,512]{0,1:T(8,128)S(1)} fusion(bf16[8192,512]{1,0:T(8,128)(2,1)} %all-gather.9.cloned.1.call-done, bf16[768,8192]{1,0:T(8,128)(2,1)} %all-gather.5.cloned.1.call-done, f32[8192]{0:T(1024)S(1)} %copy-done.1, f32[768]{0:T(1024)S(1)} %add_rsqrt_fusion), kind=kOutput, calls=%fused_computation.10 | convolution fusion | flops 6467616768 | bytes 22580224 | tf_op jit(solution)/shard_map/dot_general | solution.py:54
  210.4 0.9 copy.59
  211.9 0.9 copy.60
  213.1 2.3 fusion.51
  215.5 1.8 fusion.10
  217.9 28.3 %all-gather.11.cloned.1.call-done = bf16[512,8192]{1,0:T(8,128)(2,1)} async-done(((bf16[512,1024]{1,0:T(8,128)(2,1)}), bf16[512,8192]{1,0:T(8,128)(2,1)}) %all-gather.11.cloned.1.call-update) | async-done | bytes 8388624 | tf_op jit(solution)/shard_map/all_gather | solution.py:84
  246.2 12.9 %convolution_convert_fusion.3 = bf16[768,8192]{1,0:T(8,128)(2,1)} fusion(bf16[512,8192]{1,0:T(8,128)(2,1)} %all-gather.11.cloned.1.call-done, bf16[96,8,4,128]{3,2,1,0:T(4,128)(2,1)S(1)} %bitcast.42), kind=kOutput, calls=%fused_computation.9 | convolution fusion | flops 6448742400 | bytes 21757952 | tf_op jit(solution)/shard_map/dot_general | solution.py:82
  260.0 3.5 all-to-all-start
  263.5 90.7 %reduce-scatter.2.cloned.1.call-done = bf16[768,512]{1,0:T(8,128)(2,1)} async-done(((bf16[768,8192]{1,0:T(8,128)(2,1)}), bf16[768,512]{1,0:T(8,128)(2,1)}) %reduce-scatter.2.cloned.1.call-update) | async-done | bytes 786448 | tf_op jit(solution)/shard_map/reduce_scatter | solution.py:87
  354.2 1.4 add_convert_fusion
  356.7 1.5 reshape.257
  358.2 4.2 %all-to-all-start.1 = ((bf16[8,2,32768]{2,1,0:T(2,128)(2,1)}), bf16[8,2,32768]{2,1,0:T(2,128)(2,1)S(1)}, u32[]{:S(2)}, u32[]{:S(2)}) async-start(bf16[8,2,32768]{2,1,0:T(2,128)(2,1)} %reshape.257), calls=%async_computation.2 | async-start | bytes 2097152 | tf_op jit(solution)/shard_map/all_to_all | solution.py:140
  362.8 15.6 %all-to-all-done.1 = bf16[8,2,32768]{2,1,0:T(2,128)(2,1)S(1)} async-done(((bf16[8,2,32768]{2,1,0:T(2,128)(2,1)}), bf16[8,2,32768]{2,1,0:T(2,128)(2,1)S(1)}, u32[]{:S(2)}, u32[]{:S(2)}) %all-to-all-start.1) | async-done | bytes 1048608 | tf_op jit(solution)/shard_map/all_to_all | solution.py:140
  379.1 1.4 reshape.259
  (53 shorter events, 11.6 us)
Async XLA Ops:
  6.5 110.4 %all-gather.5.cloned.1.call-start = ((), (), s32[]{:S(2)}) async-start(), calls=%async_computation.3 | async-start | bytes 13369344 | tf_op jit(solution)/shard_map/all_gather | solution.py:50
  13.0 130.0 %copy-start.1 = (f32[8192]{0:T(1024)S(1)}, f32[8192]{0:T(1024)}, u32[]{:S(2)}) copy-start(f32[8192]{0:T(1024)} %param.10) | copy-start | bytes 98308
  14.5 128.6 %all-gather.7.cloned.1.call-start = ((), (), s32[]{:S(2)}) async-start(), calls=%async_computation.4 | async-start | bytes 2359296 | tf_op jit(solution)/shard_map/all_gather | solution.py:61
  15.2 179.5 %all-gather.9.cloned.1.call-start = ((), (), s32[]{:S(2)}) async-start(), calls=%async_computation.5 | async-start | bytes 9437184 | tf_op jit(solution)/shard_map/all_gather | solution.py:56
  16.0 230.3 %all-gather.11.cloned.1.call-start = ((), (), s32[]{:S(2)}) async-start(), calls=%async_computation.6 | async-start | bytes 9437184 | tf_op jit(solution)/shard_map/all_gather | solution.py:84
  16.5 337.7 %reduce-scatter.2.cloned.1.call-start = ((), (), s32[]{:S(2)}) async-start(), calls=%async_computation.7 | async-start | bytes 13369344 | tf_op jit(solution)/shard_map/reduce_scatter | solution.py:87
  151.9 60.8 %collective-permute-start = (bf16[768,128]{0,1:T(8,128)(2,1)S(1)}, bf16[768,128]{0,1:T(8,128)(2,1)S(1)}, u32[]{:S(2)}, u32[]{:S(2)}) collective-permute-start(bf16[768,128]{0,1:T(8,128)(2,1)S(1)} %maximum_select_fusion), channel_id=1, source_target_pairs={{0,1},{1,0},{2,3},{3,2},{4,5},{5,4},{6,7},{7,6},{8,9},{9,8},{10,11... | collective-permute-start | bytes 589832 | tf_op jit(solution)/shard_map/ppermute | solution.py:15
  259.2 95.1 %copy-start = (bf16[768,512]{1,0:T(8,128)(2,1)S(1)}, bf16[768,512]{1,0:T(8,128)(2,1)}, u32[]{:S(2)}) copy-start(bf16[768,512]{1,0:T(8,128)(2,1)} %reshape.251) | copy-start | bytes 2359300
  260.0 98.2 %all-to-all-start = ((bf16[8,1,2]{2,1,0:T(2,128)(2,1)}), bf16[8,1,2]{2,1,0:T(2,128)(2,1)S(1)}, u32[]{:S(2)}, u32[]{:S(2)}) async-start(bf16[8,1,2]{2,1,0:T(2,128)(2,1)} %reshape.265), calls=%async_computation | async-start | bytes 8192 | tf_op jit(solution)/shard_map/all_to_all | solution.py:141
  358.2 20.2 %all-to-all-start.1 = ((bf16[8,2,32768]{2,1,0:T(2,128)(2,1)}), bf16[8,2,32768]{2,1,0:T(2,128)(2,1)S(1)}, u32[]{:S(2)}, u32[]{:S(2)}) async-start(bf16[8,2,32768]{2,1,0:T(2,128)(2,1)} %reshape.257), calls=%async_computation.2 | async-start | bytes 2097152 | tf_op jit(solution)/shard_map/all_to_all | solution.py:140
Sparse Core Ops, SparseCore 0:
  14.6 102.2 all-gather.4
  118.6 24.3 all-gather.6
  144.7 49.9 all-gather.8
  196.3 49.8 all-gather.10
  259.3 94.8 reduce-scatter.1
where the time goes:
time: 388 us; the launch traced here: 387 us
  waiting for transfers between devices  297 us (77%)
  matrix products  41.1 us (11%)
  other arithmetic  14.4 us (4%)
  between operations  13.3 us (3%)
  local copies, waits for them, and re-layouts  11.6 us (3%)
  starting transfers between devices  9.68 us (2%)
    all_gather x1, waiting for transfers between devices, attention_layer(): gathered = lax.all_gather(block_rows, 'tensor', axis=1, tiled=True)  100 us
    reduce_scatter x1, waiting for transfers between devices, attention_layer(): lax.psum_scatter(terms.astype(jnp.bfloat16), 'tensor', scatter_dimension=...  90.7 us
    all_gather x1, waiting for transfers between devices, attention_layer(): lax.all_gather(query_weight, 'dp', axis=0, tiled=True)  41.1 us
    all_gather x1, waiting for transfers between devices, attention_layer(): lax.all_gather(output_weight, 'dp', axis=1, tiled=True)  28.3 us
    all_gather x1, waiting for transfers between devices, attention_layer(): lax.all_gather(keyvalue_weight, 'dp', axis=0, tiled=True)  19 us
    all_to_all x1, waiting for transfers between devices, shards(): lax.all_to_all(outgoing, 'dp', split_axis=0, concat_axis=0, tiled=True)  15.6 us
    dot_general x1, matrix products, attention_layer(): jnp.dot(rescaled_hidden, lax.all_gather(query_weight, 'dp', axis=0, tiled...  14.7 us
    dot_general x1, matrix products, attention_layer(): jnp.dot(context, lax.all_gather(output_weight, 'dp', axis=1, tiled=True),...  12.9 us
  transfers between devices with their start and end apart: 8, of which 6 were waited for; matrix products, arithmetic and copies ran while one was open for 11% of the time, Pallas kernels for 0%

commit v1 on v0

--- a/solution.py
+++ b/solution.py
@@ -117,23 +117,8 @@
     to_slot = jnp.arange(capacity_sum)[:, None] == slot_index[None, :]
     slot_flags = jnp.any(to_slot, axis=1).astype(jnp.bfloat16).reshape(group_number, slot_cap)
     item_rows = hidden.reshape(items_here, ITEM_LEN * columns)
-    kept_rank = jnp.cumsum(staying) - staying
-    pick_own = (jnp.arange(most_kept)[:, None] == kept_rank[None, :]) & (staying[None, :] == 1)
-    local_records = jnp.dot(
-        pick_own.astype(jnp.bfloat16), item_rows, preferred_element_type=jnp.float32
-    ).astype(jnp.bfloat16)
-    finished = attention_layer(
-        local_records.reshape(most_kept * ITEM_LEN, columns),
-        norm_gain,
-        query_weight,
-        keyvalue_weight,
-        output_weight,
-    )
-    slot_from_kept = jnp.dot(to_slot.astype(jnp.float32), pick_own.astype(jnp.float32).T)
     outgoing = jnp.dot(
-        slot_from_kept.astype(jnp.bfloat16),
-        finished.reshape(most_kept, ITEM_LEN * columns),
-        preferred_element_type=jnp.float32,
+        to_slot.astype(jnp.bfloat16), item_rows, preferred_element_type=jnp.float32
     ).astype(jnp.bfloat16)
     outgoing = outgoing.reshape(group_number, slot_cap, ITEM_LEN * columns)
     arrived, arrived_flags = (
@@ -145,7 +130,13 @@
         arrived_flags.reshape(capacity_sum),
         taken,
     )
-    return compact.reshape(taken * ITEM_LEN, columns)
+    return attention_layer(
+        compact.reshape(taken * ITEM_LEN, columns),
+        norm_gain,
+        query_weight,
+        keyvalue_weight,
+        output_weight,
+    )
 
 
 def solution(mesh):

time: 388 us -> 339 us (0.87)
  waiting for transfers between devices: 297 us -> 272 us
  matrix products: 41.1 us -> 26 us
  other arithmetic: 14.4 us -> 9.84 us
  local copies, waits for them, and re-layouts: 11.6 us -> 7.57 us
    all_gather x1, waiting for transfers between devices: 100 us -> 66.5 us  [attention_layer(): gathered = lax.all_gather(block_rows, 'tensor', axis=1, tiled=True)]
    dot_general x3 -> x2, matrix products: 15.7 us -> 0.99 us  [the longest x1 0.58 us: attend(): jnp.einsum('nlhd,nmd->nhlm', request_vectors, keys_part, preferred_elemen...]
    all_gather x1, waiting for transfers between devices: 28.3 us -> 38.8 us  [attention_layer(): lax.all_gather(output_weight, 'dp', axis=1, tiled=True)]
    reshape x0 -> x1, matrix products: none -> 9.3 us  [attention_layer(): query_accumulated.reshape(row_count, head_count, HD)]
    reduce_scatter x1, waiting for transfers between devices: 90.7 us -> 81.9 us  [attention_layer(): lax.psum_scatter(terms.astype(jnp.bfloat16), 'tensor', scatter_dimension=...]
    dot_general x1, matrix products: 12.9 us -> 8.82 us  [attention_layer(): jnp.dot(context, lax.all_gather(output_weight, 'dp', axis=1, tiled=True),...]
  transfers between devices with their start and end apart: 8 -> 8, of which waited for: 6 -> 8; matrix products, arithmetic and copies ran while one was open for 11% -> 8% of each run, Pallas kernels for 0% -> 0%
where the time goes in v1:
time: 339 us
  waiting for transfers between devices  272 us (80%)
  matrix products  26 us (8%)
  between operations  13.3 us (4%)
  starting transfers between devices  9.88 us (3%)
  other arithmetic  9.84 us (3%)
  local copies, waits for them, and re-layouts  7.57 us (2%)
    reduce_scatter x1, waiting for transfers between devices, attention_layer(): lax.psum_scatter(terms.astype(jnp.bfloat16), 'tensor', scatter_dimension=...  81.9 us
    all_gather x1, waiting for transfers between devices, attention_layer(): gathered = lax.all_gather(block_rows, 'tensor', axis=1, tiled=True)  66.5 us
    all_gather x1, waiting for transfers between devices, attention_layer(): lax.all_gather(query_weight, 'dp', axis=0, tiled=True)  40.2 us
    all_gather x1, waiting for transfers between devices, attention_layer(): lax.all_gather(output_weight, 'dp', axis=1, tiled=True)  38.8 us
    all_gather x1, waiting for transfers between devices, attention_layer(): lax.all_gather(keyvalue_weight, 'dp', axis=0, tiled=True)  22 us
    all_to_all x1, waiting for transfers between devices, shards(): lax.all_to_all(outgoing, 'dp', split_axis=0, concat_axis=0, tiled=True)  15.5 us
    reshape x1, matrix products, attention_layer(): query_accumulated.reshape(row_count, head_count, HD)  9.3 us
    dot_general x1, matrix products, attention_layer(): jnp.dot(context, lax.all_gather(output_weight, 'dp', axis=1, tiled=True),...  8.82 us
  transfers between devices with their start and end apart: 8, of which 8 were waited for; matrix products, arithmetic and copies ran while one was open for 8% of the time, Pallas kernels for 0%

profile of v1, /device:TPU:0, one launch (start us, length us, event | category | flops | bytes accessed | tf_op | source)
XLA Modules:
  0.0 338.5 jit_solution(16181220857794969225)
XLA Ops:
  7.2 0.7 fusion.22
  8.0 0.8 fusion.20
  9.6 0.7 reshape.226
  10.3 4.4 %all-to-all-start = ((bf16[8,1,2]{2,1,0:T(2,128)(2,1)}), bf16[8,1,2]{2,1,0:T(2,128)(2,1)S(1)}, u32[]{:S(2)}, u32[]{:S(2)}) async-start(bf16[8,1,2]{2,1,0:T(2,128)(2,1)} %reshape.226), calls=%async_computation | async-start | bytes 8192 | tf_op jit(solution)/shard_map/all_to_all | solution.py:126
  14.7 1.6 reshape.213
  16.6 1.5 reshape.214
  18.2 1.7 all-to-all-done
  19.9 3.6 %all-to-all-start.1 = ((bf16[8,2,32768]{2,1,0:T(2,128)(2,1)}), bf16[8,2,32768]{2,1,0:T(2,128)(2,1)S(1)}, u32[]{:S(2)}, u32[]{:S(2)}) async-start(bf16[8,2,32768]{2,1,0:T(2,128)(2,1)} %reshape.214), calls=%async_computation.1 | async-start | bytes 2097152 | tf_op jit(solution)/shard_map/all_to_all | solution.py:125
  23.8 15.5 %all-to-all-done.1 = bf16[8,2,32768]{2,1,0:T(2,128)(2,1)S(1)} async-done(((bf16[8,2,32768]{2,1,0:T(2,128)(2,1)}), bf16[8,2,32768]{2,1,0:T(2,128)(2,1)S(1)}, u32[]{:S(2)}, u32[]{:S(2)}) %all-to-all-start.1) | async-done | bytes 1048608 | tf_op jit(solution)/shard_map/all_to_all | solution.py:125
  40.0 1.4 reshape.216
  41.5 0.7 all-gather.7.cloned.1.call-update
  42.2 0.7 all-gather.9.cloned.1.call-update
  43.6 66.5 %all-gather.5.cloned.1.call-done = bf16[384,8192]{1,0:T(8,128)(2,1)} async-done(((bf16[384,512]{1,0:T(8,128)(2,1)}), bf16[384,8192]{1,0:T(8,128)(2,1)}) %all-gather.5.cloned.1.call-update) | async-done | bytes 6291472 | tf_op jit(solution)/shard_map/all_gather | solution.py:50
  110.1 4.1 %fusion.1 = f32[384]{0:T(512)S(1)} fusion(bf16[384,8192]{1,0:T(8,128)(2,1)} %all-gather.5.cloned.1.call-done), kind=kLoop, calls=%fused_computation.5 | loop fusion | flops 9436800 | bytes 6292992 | tf_op jit(solution)/shard_map/reduce_sum | solution.py:52
  114.2 22.0 %all-gather.7.cloned.1.call-done = bf16[8192,128]{1,0:T(8,128)(2,1)} async-done(((bf16[1024,128]{1,0:T(8,128)(2,1)}), bf16[8192,128]{1,0:T(8,128)(2,1)}) %all-gather.7.cloned.1.call-update) | async-done | bytes 2097168 | tf_op jit(solution)/shard_map/all_gather | solution.py:61
  136.2 5.6 %fusion.6 = f32[384,128]{0,1:T(8,128)S(1)} fusion(bf16[8192,128]{1,0:T(8,128)(2,1)} %all-gather.7.cloned.1.call-done, bf16[384,8192]{1,0:T(8,128)(2,1)} %all-gather.5.cloned.1.call-done, f32[8192]{0:T(1024)S(1)} %copy-done.1, f32[384]{0:T(512)S(1)} %add_rsqrt_fusion), kind=kOutput, calls=%fused_computation.10 | convolution fusion | flops 817889280 | bytes 8619520 | tf_op jit(solution)/shard_map/dot_general | solution.py:59
  142.2 1.7 collective-permute-start
  144.0 3.5 %collective-permute-done = bf16[384,128]{0,1:T(8,128)(2,1)S(1)} collective-permute-done((bf16[384,128]{0,1:T(8,128)(2,1)S(1)}, bf16[384,128]{0,1:T(8,128)(2,1)S(1)}, u32[]{:S(2)}, u32[]{:S(2)}) %collective-permute-start) | collective-permute-done | bytes 98336 | tf_op jit(solution)/shard_map/ppermute | solution.py:15
  147.7 40.2 %all-gather.9.cloned.1.call-done = bf16[8192,512]{1,0:T(8,128)(2,1)} async-done(((bf16[1024,512]{1,0:T(8,128)(2,1)}), bf16[8192,512]{1,0:T(8,128)(2,1)}) %all-gather.9.cloned.1.call-update) | async-done | bytes 8388624 | tf_op jit(solution)/shard_map/all_gather | solution.py:56
  188.0 9.3 %fusion.4 = f32[384,512]{0,1:T(8,128)S(1)} fusion(bf16[8192,512]{1,0:T(8,128)(2,1)} %all-gather.9.cloned.1.call-done, bf16[384,8192]{1,0:T(8,128)(2,1)} %all-gather.5.cloned.1.call-done, f32[8192]{0:T(1024)S(1)} %copy-done.1, f32[384]{0:T(512)S(1)} %add_rsqrt_fusion), kind=kOutput, calls=%fused_computation.9 | convolution fusion | flops 3233808384 | bytes 15500800 | tf_op jit(solution)/shard_map/reshape | solution.py:67
  200.7 38.8 %all-gather.11.cloned.1.call-done = bf16[512,8192]{1,0:T(8,128)(2,1)} async-done(((bf16[512,1024]{1,0:T(8,128)(2,1)}), bf16[512,8192]{1,0:T(8,128)(2,1)}) %all-gather.11.cloned.1.call-update) | async-done | bytes 8388624 | tf_op jit(solution)/shard_map/all_gather | solution.py:84
  239.4 8.8 %convolution_convert_fusion.2 = bf16[384,8192]{1,0:T(8,128)(2,1)} fusion(bf16[512,8192]{1,0:T(8,128)(2,1)} %all-gather.11.cloned.1.call-done, bf16[48,8,4,128]{3,2,1,0:T(4,128)(2,1)S(1)} %bitcast.41), kind=kOutput, calls=%fused_computation.8 | convolution fusion | flops 3224371200 | bytes 15073280 | tf_op jit(solution)/shard_map/dot_general | solution.py:82
  248.3 81.9 %reduce-scatter.2.cloned.1.call-done = bf16[384,512]{1,0:T(8,128)(2,1)} async-done(((bf16[384,8192]{1,0:T(8,128)(2,1)}), bf16[384,512]{1,0:T(8,128)(2,1)}) %reduce-scatter.2.cloned.1.call-update) | async-done | bytes 393232 | tf_op jit(solution)/shard_map/reduce_scatter | solution.py:87
  330.2 1.8 add_convert_fusion
  (46 shorter events, 7.9 us)
Async XLA Ops:
  10.3 9.6 %all-to-all-start = ((bf16[8,1,2]{2,1,0:T(2,128)(2,1)}), bf16[8,1,2]{2,1,0:T(2,128)(2,1)S(1)}, u32[]{:S(2)}, u32[]{:S(2)}) async-start(bf16[8,1,2]{2,1,0:T(2,128)(2,1)} %reshape.226), calls=%async_computation | async-start | bytes 8192 | tf_op jit(solution)/shard_map/all_to_all | solution.py:126
  18.2 118.0 %copy-start.1 = (f32[8192]{0:T(1024)S(1)}, f32[8192]{0:T(1024)}, u32[]{:S(2)}) copy-start(f32[8192]{0:T(1024)} %param.10) | copy-start | bytes 98308
  19.9 19.4 %all-to-all-start.1 = ((bf16[8,2,32768]{2,1,0:T(2,128)(2,1)}), bf16[8,2,32768]{2,1,0:T(2,128)(2,1)S(1)}, u32[]{:S(2)}, u32[]{:S(2)}) async-start(bf16[8,2,32768]{2,1,0:T(2,128)(2,1)} %reshape.214), calls=%async_computation.1 | async-start | bytes 2097152 | tf_op jit(solution)/shard_map/all_to_all | solution.py:125
  23.4 86.6 %all-gather.5.cloned.1.call-start = ((), (), s32[]{:S(2)}) async-start(), calls=%async_computation.3 | async-start | bytes 6684672 | tf_op jit(solution)/shard_map/all_gather | solution.py:50
  41.4 94.7 %all-gather.7.cloned.1.call-start = ((), (), s32[]{:S(2)}) async-start(), calls=%async_computation.4 | async-start | bytes 2359296 | tf_op jit(solution)/shard_map/all_gather | solution.py:61
  42.2 145.8 %all-gather.9.cloned.1.call-start = ((), (), s32[]{:S(2)}) async-start(), calls=%async_computation.5 | async-start | bytes 9437184 | tf_op jit(solution)/shard_map/all_gather | solution.py:56
  42.9 196.5 %all-gather.11.cloned.1.call-start = ((), (), s32[]{:S(2)}) async-start(), calls=%async_computation.6 | async-start | bytes 9437184 | tf_op jit(solution)/shard_map/all_gather | solution.py:84
  43.5 286.7 %reduce-scatter.2.cloned.1.call-start = ((), (), s32[]{:S(2)}) async-start(), calls=%async_computation.7 | async-start | bytes 6684672 | tf_op jit(solution)/shard_map/reduce_scatter | solution.py:87
  142.2 5.2 %collective-permute-start = (bf16[384,128]{0,1:T(8,128)(2,1)S(1)}, bf16[384,128]{0,1:T(8,128)(2,1)S(1)}, u32[]{:S(2)}, u32[]{:S(2)}) collective-permute-start(bf16[384,128]{0,1:T(8,128)(2,1)S(1)} %maximum_select_fusion), channel_id=1, source_target_pairs={{0,1},{1,0},{2,3},{3,2},{4,5},{5,4},{6,7},{7,6},{8,9},{9,8},{10,11... | collective-permute-start | bytes 294920 | tf_op jit(solution)/shard_map/ppermute | solution.py:15
  239.4 90.8 %copy-start = (bf16[384,512]{1,0:T(8,128)(2,1)S(1)}, bf16[384,512]{1,0:T(8,128)(2,1)}, u32[]{:S(2)}) copy-start(bf16[384,512]{1,0:T(8,128)(2,1)} %reshape.216) | copy-start | bytes 1179652
Sparse Core Ops, SparseCore 0:
  41.5 68.4 all-gather.4
  111.8 24.3 all-gather.6
  137.9 50.0 all-gather.8
  189.5 49.8 all-gather.10
  248.4 81.7 reduce-scatter.1

commit v2 on v1

v2 whole, which is shorter than its diff:
```python
import functools

import jax
import jax.numpy as jnp
import numpy as np
from jax import lax
from jax.experimental import pallas as pl
from jax.experimental.pallas import tpu as pltpu
from jax.sharding import PartitionSpec as P

MESH = pl.DeviceIdType.MESH

HD = 128
ITEM_LEN = 64
HERE = 16
TAKEN = 6
ROWS = TAKEN * ITEM_LEN
WIDE = 512
DEPTH = 1024
EPSILON = 1e-05
THETA = 500000.0
BF = jnp.bfloat16
F32 = jnp.float32

PIECE = DEPTH // 4
HALF = ROWS // 2
QUARTER = ROWS // 4


def tables():
    j = np.arange(HD // 2, dtype=np.float64)
    freq = (THETA ** (-2.0 * j / HD)).astype(np.float32)
    phase = (np.arange(ITEM_LEN, dtype=np.float32)[:, None] * freq).astype(np.float64)
    cos, sin = np.cos(phase), np.sin(phase)
    return (
        np.concatenate([cos, cos], axis=1).astype(np.float32),
        np.concatenate([-sin, sin], axis=1).astype(np.float32),
    )


def kernel(
    exited, destination, hidden, gain, wq, wkv, wo, cos, sin, out,
    hid, outgoing, arrived, meta, meta_scalar, act, wbuf, obuf, acc, squares, qs, kvown, kvpart,
    ctx, part, r1, r2, s1, q1, q2,
    local_sem, meta_s, meta_r, route_s, route_r, x_s, x_r, ag_s, ag_r, rs_s, rs_r, kv_s, kv_r,
):
    me = lax.axis_index("dp")
    t = lax.axis_index("tensor")
    x, c = me // 2, me % 2
    z, y = t // 4, t % 4
    left = ((x + 3) % 4) * 2 + c
    right = ((x + 1) % 4) * 2 + c
    far = ((x + 2) % 4) * 2 + c
    zp, zm, zf = (z + 1) % 4, (z + 3) % 4, (z + 2) % 4
    yp, ym, yf = (y + 1) % 4, (y + 3) % 4, (y + 2) % 4

    def sibling(i):
        return i + 1 - 2 * c

    sib = sibling(me)

    started = []

    def put(src, dst, send, recv, device):
        copy = pltpu.make_async_remote_copy(
            src_ref=src, dst_ref=dst, send_sem=send, recv_sem=recv,
            device_id=device, device_id_type=MESH,
        )
        copy.start()
        started.append(copy)

    def got(dst, recv):
        pltpu.make_async_remote_copy(
            src_ref=dst, dst_ref=dst, send_sem=recv, recv_sem=recv,
            device_id=(sib, t), device_id_type=MESH,
        ).wait_recv()

    loads = [pltpu.make_async_copy(hidden, hid, local_sem.at[0])]
    loads.append(pltpu.make_async_copy(wq, wbuf.at[me, :, pl.ds(0, WIDE)], local_sem.at[1]))
    loads.append(pltpu.make_async_copy(wkv, wbuf.at[me, :, pl.ds(WIDE, HD)], local_sem.at[2]))
    for s in range(4):
        for h in range(2):
            loads.append(
                pltpu.make_async_copy(
                    wo.at[:, pl.ds(h * WIDE + s * HD, HD)],
                    obuf.at[s, me, :, pl.ds(h * HD, HD)],
                    local_sem.at[3 + 2 * s + h],
                )
            )
    for load in loads:
        load.start()

    barrier = pltpu.get_barrier_semaphore()
    peers = [((me + k) % 8, t) for k in range(1, 8)]
    peers += [(me, zp * 4 + y), (me, zm * 4 + y), (me, z * 4 + yp), (me, z * 4 + ym)]
    for peer in peers:
        pl.semaphore_signal(barrier, inc=1, device_id=peer, device_id_type=MESH)
    pl.semaphore_wait(barrier, len(peers))

    codes = [jnp.where(exited[k] == 0, destination[k], -1) for k in range(HERE)]
    lane = lax.broadcasted_iota(jnp.int32, (8, 128), 1)
    row = jnp.full((8, 128), -1, jnp.int32)
    for k in range(HERE):
        row = jnp.where(lane == k, codes[k], row)
    meta[me] = row
    for k in range(1, 8):
        put(meta.at[me], meta.at[me], meta_s.at[k], meta_r.at[k], ((me + k) % 8, t))

    loads[0].wait()
    for k in [4, 2, 6, 3, 5, 1, 7, 0]:
        dest = (me + k) % 8 if k else me
        seen = jnp.int32(0)
        first = jnp.int32(0)
        second = jnp.int32(0)
        for item in range(HERE):
            hit = codes[item] == dest
            first = jnp.where(hit & (seen == 0), item, first)
            second = jnp.where(hit & (seen == 1), item, second)
            seen = seen + jnp.where(hit, 1, 0)
        if k:
            outgoing[dest, 0] = hid[first]
            outgoing[dest, 1] = hid[second]
            put(outgoing.at[dest], arrived.at[me], route_s.at[k], route_r.at[k], (dest, t))
        else:
            arrived[me, 0] = hid[first]
            arrived[me, 1] = hid[second]
    for load in loads[1:]:
        load.wait()

    def weights(r, i, low=0, count=None):
        if r < 4:
            return wbuf.at[i, pl.ds(r * PIECE + low, count or PIECE), :]
        return obuf.at[r - 4, i, pl.ds(low, count or WIDE), :]

    def half_of(r):
        return PIECE // 2 if r < 4 else WIDE // 2

    def x_put(r, k, view, device):
        put(view, view, x_s.at[r, k], x_r.at[r, k], (device, t))

    def x_own_sibling(r):
        x_put(r, 4, weights(r, me), sib)

    def x_own(r):
        x_put(r, 0, weights(r, me), right)
        x_put(r, 1, weights(r, me), left)

    def x_near(r):
        n = half_of(r)
        got(weights(r, left), x_r.at[r, 0])
        x_put(r, 2, weights(r, left, 0, n), right)
        x_put(r, 5, weights(r, left), sib)
        got(weights(r, right), x_r.at[r, 1])
        x_put(r, 3, weights(r, right, n, n), left)
        x_put(r, 6, weights(r, right), sib)

    def x_far(r):
        n = half_of(r)
        got(weights(r, far, 0, n), x_r.at[r, 2])
        x_put(r, 7, weights(r, far, 0, n), sib)
        got(weights(r, far, n, n), x_r.at[r, 3])
        x_put(r, 8, weights(r, far, n, n), sib)

    def x_sibling(r):
        n = half_of(r)
        got(weights(r, sib), x_r.at[r, 4])
        got(weights(r, sibling(left)), x_r.at[r, 5])
        got(weights(r, sibling(right)), x_r.at[r, 6])
        got(weights(r, sibling(far), 0, n), x_r.at[r, 7])
        got(weights(r, sibling(far), n, n), x_r.at[r, 8])

    for r in range(8):
        x_own_sibling(r)

    for k in range(1, 8):
        got(meta.at[(me + 8 - k) % 8], meta_r.at[k])
    to_scalar = pltpu.make_async_copy(meta, meta_scalar, local_sem.at[11])
    to_scalar.start()
    to_scalar.wait()
    picks = [jnp.int32(0)] * TAKEN
    rank = jnp.int32(0)
    for j in range(8):
        count = jnp.int32(0)
        for item in range(HERE):
            count = count + jnp.where(meta_scalar[j, 0, item] == me, 1, 0)
        for s in range(2):
            valid = count > s
            for r in range(TAKEN):
                picks[r] = jnp.where(valid & (rank == r), 2 * j + s, picks[r])
            rank = rank + jnp.where(valid, 1, 0)

    for k in range(1, 8):
        got(arrived.at[(me + 8 - k) % 8], route_r.at[k])
    flat = arrived.reshape(16, ITEM_LEN, WIDE)
    for r in range(TAKEN):
        act[t, pl.ds(r * ITEM_LEN, ITEM_LEN), :] = flat[picks[r]]

    def line(half, phase):
        along_z = (half == 0) == (phase == 0)
        if along_z:
            return (z, zm, zp, zf), lambda a, b: a * 4 + b
        return (y, ym, yp, yf), lambda a, b: b * 4 + a

    def chunk(tt, half, low=0, count=HALF):
        return act.at[tt, pl.ds(half * HALF + low, count), :]

    def ag_put(half, k, view, device):
        put(view, view, ag_s.at[half, k], ag_r.at[half, k], (me, device))

    def other(half):
        return y if half == 0 else z

    def ag_send(half, phase, base, tt, near):
        (own, minus, plus, opposite), at = line(half, phase)
        place = other(half) if phase == 0 else near
        ag_put(half, base, chunk(tt, half), at(plus, place))
        ag_put(half, base + 1, chunk(tt, half), at(minus, place))

    def ag_near(half, phase, base, place):
        (own, minus, plus, opposite), at = line(half, phase)
        got(chunk(at(minus, place), half), ag_r.at[half, base])
        q = HALF // 2
        here = other(half) if phase == 0 else (z if half == 0 else y)
        ag_put(half, base + 2, chunk(at(minus, place), half, 0, q), at(plus, here))
        got(chunk(at(plus, place), half), ag_r.at[half, base + 1])
        ag_put(half, base + 3, chunk(at(plus, place), half, q, q), at(minus, here))

    def ag_far(half, phase, base, place):
        (own, minus, plus, opposite), at = line(half, phase)
        q = HALF // 2
        got(chunk(at(opposite, place), half, 0, q), ag_r.at[half, base + 2])
        got(chunk(at(opposite, place), half, q, q), ag_r.at[half, base + 3])

    def places(half):
        return (z, zm, zp, zf) if half == 0 else (y, ym, yp, yf)

    def first_at(half, a):
        return a * 4 + y if half == 0 else z * 4 + a

    def ag2_send(half, n):
        a = places(half)[n]
        ag_send(half, 1, 4 + 4 * n, first_at(half, a), places(half)[0])

    def ag2_near(half, n):
        ag_near(half, 1, 4 + 4 * n, places(half)[n])

    def ag2_far(half, n):
        ag_far(half, 1, 4 + 4 * n, places(half)[n])

    for half in range(2):
        ag_send(half, 0, 0, t, None)
    x_own(0)
    for half in range(2):
        ag2_send(half, 0)
    x_own(1)
    for half in range(2):
        ag_near(half, 0, 0, other(half))
        ag2_send(half, 1)
        ag2_send(half, 2)
    x_near(0)
    for half in range(2):
        ag_far(half, 0, 0, other(half))
        ag2_send(half, 3)
    for half in range(2):
        ag2_near(half, 0)
    x_far(0)
    x_own(2)
    x_near(1)
    for half in range(2):
        ag2_near(half, 1)
    for half in range(2):
        ag2_near(half, 2)
    x_far(1)
    x_own(3)
    x_near(2)
    for half in range(2):
        ag2_near(half, 3)
    for n in range(4):
        for half in range(2):
            ag2_far(half, n)

    acc[...] = jnp.zeros_like(acc)
    squares[...] = jnp.zeros_like(squares)

    def project(p):
        x_sibling(p)

        @pl.loop(0, 8)
        def _(i):
            tt = 2 * i + p // 2
            cols = pl.ds((p % 2) * PIECE, PIECE)
            rows = act[tt, :, cols].astype(F32)
            power = rows * rows
            squares[...] += power[:, :HD] + power[:, HD:]
            scaled = (rows * gain[tt, :, cols]).astype(BF)
            acc[...] += jnp.dot(
                scaled, wbuf[i, pl.ds(p * PIECE, PIECE), :], preferred_element_type=F32
            )

    project(0)
    x_far(2)
    x_own(4)
    x_near(3)
    project(1)
    project(2)
    x_far(3)
    x_own(5)
    x_near(4)
    project(3)

    def rotated(value):
        return value * cos[...] + pltpu.roll(value, HD // 2, 1) * sin[...]

    squares[:, :1] = lax.rsqrt(
        jnp.sum(squares[...], axis=1, keepdims=True) * (1.0 / (16 * WIDE)) + EPSILON
    )
    parity = t % 2

    @pl.loop(0, TAKEN)
    def _(n):
        rows = pl.ds(n * ITEM_LEN, ITEM_LEN)
        value = acc[rows, pl.ds(WIDE, HD)] * squares[rows, :1]
        kvown[rows, :] = jnp.where(parity == 0, rotated(value), value).astype(BF)

    put(kvown, kvpart, kv_s, kv_r, (me, t + 1 - 2 * parity))

    @pl.loop(0, TAKEN)
    def _(n):
        rows = pl.ds(n * ITEM_LEN, ITEM_LEN)
        inverse = squares[rows, :1]
        for h in range(4):
            value = acc[rows, pl.ds(h * HD, HD)] * inverse
            qs[n, pl.ds(h * ITEM_LEN, ITEM_LEN), :] = rotated(value).astype(BF)

    got(kvpart, kv_r)

    @pl.loop(0, TAKEN)
    def _(n):
        rows = pl.ds(n * ITEM_LEN, ITEM_LEN)
        mine, theirs = kvown[rows, :], kvpart[rows, :]
        keys = jnp.where(parity == 0, mine, theirs)
        values = jnp.where(parity == 0, theirs, mine)
        scores = lax.dot_general(
            qs[n], keys, (((1,), (1,)), ((), ())), preferred_element_type=F32
        ) * (HD ** -0.5)
        place = lax.broadcasted_iota(jnp.int32, scores.shape, 0) % ITEM_LEN
        scores = jnp.where(
            place >= lax.broadcasted_iota(jnp.int32, scores.shape, 1), scores, -1e30
        )
        raised = jnp.exp(scores - jnp.max(scores, axis=1, keepdims=True))
        probs = (raised * (1.0 / jnp.sum(raised, axis=1, keepdims=True))).astype(BF)
        context = jnp.dot(probs, values, preferred_element_type=F32).astype(BF)
        for h in range(4):
            ctx[rows, pl.ds(h * HD, HD)] = context[h * ITEM_LEN:(h + 1) * ITEM_LEN, :]

    def multiply(s):
        x_sibling(4 + s)

        @pl.loop(0, 4)
        def _(a):
            for b in range(2):
                term = jnp.dot(
                    ctx[...], obuf[s, 2 * a + b], preferred_element_type=F32
                ).astype(BF)
                part[s, a, 2 * b] = term[:, :HD]
                part[s, a, 2 * b + 1] = term[:, HD:]

    def rs_put(s, half, k, src, dst, device):
        put(src, dst, rs_s.at[s, half, k], rs_r.at[s, half, k], (me, device))

    A = (0, QUARTER)
    B = (QUARTER, QUARTER)

    def block(s, half, a, rows):
        low, count = rows
        span = pl.ds(half * HALF + low, count)
        if half == 0:
            return part.at[s, a, :, span, :]
        return part.at[s, :, a, span, :]

    def devices(half, phase):
        if (half == 0) == (phase == 0):
            return zp * 4 + y, zm * 4 + y
        return z * 4 + yp, z * 4 + ym

    def ends(half, phase):
        if (half == 0) == (phase == 0):
            return z, zm, zp, zf
        return y, ym, yp, yf

    def span(rows):
        return pl.ds(rows[0], rows[1])

    def send_first(s):
        for half in range(2):
            own, minus, plus, opposite = ends(half, 0)
            up, down = devices(half, 0)
            rs_put(s, half, 0, block(s, half, opposite, A), r1.at[s, half, 0], up)
            rs_put(s, half, 1, block(s, half, opposite, B), r1.at[s, half, 1], down)
            rs_put(s, half, 2, block(s, half, plus, B), r2.at[s, half, 0, :, span(B), :], up)
            rs_put(s, half, 3, block(s, half, minus, A), r2.at[s, half, 1, :, span(A), :], down)

    def add_first(s):
        for half in range(2):
            own, minus, plus, opposite = ends(half, 0)
            up, down = devices(half, 0)
            for side, (a, rows, device) in enumerate(((plus, A, up), (minus, B, down))):
                got(r1.at[s, half, side], rs_r.at[s, half, side])
                view = block(s, half, a, rows)
                view[...] = (view[...].astype(F32) + r1[s, half, side].astype(F32)).astype(BF)
                rs_put(s, half, 4 + side, view, r2.at[s, half, side, :, span(rows), :], device)

    def send_second(s):
        for half in range(2):
            own, minus, plus, opposite = ends(half, 0)
            got(r2.at[s, half, 0, :, span(B), :], rs_r.at[s, half, 2])
            got(r2.at[s, half, 1, :, span(A), :], rs_r.at[s, half, 3])
            got(r2.at[s, half, 0, :, span(A), :], rs_r.at[s, half, 4])
            got(r2.at[s, half, 1, :, span(B), :], rs_r.at[s, half, 5])
            view = block(s, half, own, (0, HALF))
            s1[s, half] = (
                view[...].astype(F32) + r2[s, half, 0].astype(F32) + r2[s, half, 1].astype(F32)
            ).astype(BF)
            own, minus, plus, opposite = ends(half, 1)
            up, down = devices(half, 1)
            to = lambda a, rows: s1.at[s, half, a, span(rows), :]
            rs_put(s, half, 6, to(opposite, A), q1.at[s, half, 0], up)
            rs_put(s, half, 7, to(opposite, B), q1.at[s, half, 1], down)
            rs_put(s, half, 8, to(plus, B), q2.at[s, half, 0, span(B), :], up)
            rs_put(s, half, 9, to(minus, A), q2.at[s, half, 1, span(A), :], down)

    def add_second(s):
        for half in range(2):
            own, minus, plus, opposite = ends(half, 1)
            up, down = devices(half, 1)
            for side, (a, rows, device) in enumerate(((plus, A, up), (minus, B, down))):
                got(q1.at[s, half, side], rs_r.at[s, half, 6 + side])
                view = s1.at[s, half, a, span(rows), :]
                view[...] = (view[...].astype(F32) + q1[s, half, side].astype(F32)).astype(BF)
                rs_put(s, half, 10 + side, view, q2.at[s, half, side, span(rows), :], device)

    def finish(s):
        for half in range(2):
            own, minus, plus, opposite = ends(half, 1)
            got(q2.at[s, half, 0, span(B), :], rs_r.at[s, half, 8])
            got(q2.at[s, half, 1, span(A), :], rs_r.at[s, half, 9])
            got(q2.at[s, half, 0, span(A), :], rs_r.at[s, half, 10])
            got(q2.at[s, half, 1, span(B), :], rs_r.at[s, half, 11])
            rows, cols = pl.ds(half * HALF, HALF), pl.ds(s * HD, HD)
            out[rows, cols] = (
                act[t, rows, cols].astype(F32)
                + s1[s, half, own].astype(F32)
                + q2[s, half, 0].astype(F32)
                + q2[s, half, 1].astype(F32)
            ).astype(BF)

    x_far(4)
    x_own(6)
    x_near(5)
    multiply(0)
    send_first(0)
    x_far(5)
    x_own(7)
    x_near(6)
    add_first(0)
    multiply(1)
    send_first(1)
    send_second(0)
    add_first(1)
    x_far(6)
    x_near(7)
    add_second(0)
    multiply(2)
    send_first(2)
    send_second(1)
    add_first(2)
    x_far(7)
    finish(0)
    add_second(1)
    multiply(3)
    send_first(3)
    send_second(2)
    add_first(3)
    finish(1)
    add_second(2)
    send_second(3)
    finish(2)
    add_second(3)
    finish(3)

    for copy in started:
        copy.wait_send()


def shards(hidden, exited, destination, norm_gain, query_weight, keyvalue_weight, output_weight):
    cos, sin = tables()
    smem = pl.BlockSpec(memory_space=pltpu.SMEM)
    vmem = pl.BlockSpec(memory_space=pltpu.VMEM)
    hbm = pl.BlockSpec(memory_space=pl.ANY)
    dma = pltpu.SemaphoreType.DMA
    return pl.pallas_call(
        kernel,
        out_shape=jax.ShapeDtypeStruct((ROWS, WIDE), BF),
        in_specs=[smem, smem, hbm, vmem, hbm, hbm, hbm, vmem, vmem],
        out_specs=vmem,
        scratch_shapes=[
            pltpu.VMEM((HERE, ITEM_LEN, WIDE), BF),
            pltpu.VMEM((8, 2, ITEM_LEN, WIDE), BF),
            pltpu.VMEM((8, 2, ITEM_LEN, WIDE), BF),
            pltpu.VMEM((8, 8, 128), jnp.int32),
            pltpu.SMEM((8, 8, 128), jnp.int32),
            pltpu.VMEM((16, ROWS, WIDE), BF),
            pltpu.VMEM((8, DEPTH, WIDE + HD), BF),
            pltpu.VMEM((4, 8, WIDE, 2 * HD), BF),
            pltpu.VMEM((ROWS, WIDE + HD), F32),
            pltpu.VMEM((ROWS, HD), F32),
            pltpu.VMEM((TAKEN, 4 * ITEM_LEN, HD), BF),
            pltpu.VMEM((ROWS, HD), BF),
            pltpu.VMEM((ROWS, HD), BF),
            pltpu.VMEM((ROWS, WIDE), BF),
            pltpu.VMEM((4, 4, 4, ROWS, HD), BF),
            pltpu.VMEM((4, 2, 2, 4, QUARTER, HD), BF),
            pltpu.VMEM((4, 2, 2, 4, HALF, HD), BF),
            pltpu.VMEM((4, 2, 4, HALF, HD), BF),
            pltpu.VMEM((4, 2, 2, QUARTER, HD), BF),
            pltpu.VMEM((4, 2, 2, HALF, HD), BF),
            dma((12,)),
            dma((8,)),
            dma((8,)),
            dma((8,)),
            dma((8,)),
            dma((8, 9)),
            dma((8, 9)),
            dma((2, 20)),
            dma((2, 20)),
            dma((4, 2, 12)),
            dma((4, 2, 12)),
            dma(()),
            dma(()),
        ],
        compiler_params=pltpu.CompilerParams(
            collective_id=0, has_side_effects=True, vmem_limit_bytes=60 * 1024 * 1024
        ),
        cost_estimate=pl.CostEstimate(
            flops=2 * ROWS * 16 * WIDE * (2 * WIDE + HD),
            bytes_accessed=8 * 1024 * 1024,
            transcendentals=ROWS * 4 * ITEM_LEN,
        ),
    )(
        exited,
        destination,
        hidden.reshape(HERE, ITEM_LEN, WIDE),
        norm_gain.reshape(16, 1, WIDE),
        query_weight,
        keyvalue_weight,
        output_weight,
        jnp.asarray(cos),
        jnp.asarray(sin),
    )


def solution(mesh):
    placed = (
        P("dp", "tensor"),
        P("dp"),
        P("dp"),
        P(),
        P("dp", "tensor"),
        P("dp", "tensor"),
        P("tensor", "dp"),
    )
    return jax.shard_map(
        shards, mesh=mesh, in_specs=placed, out_specs=P("dp", "tensor"), check_vma=False
    )
```

time: 339 us -> 147 us (0.43)
  waiting for transfers between devices: 272 us -> 0 us
  Pallas kernels: 0 us -> 145 us
  matrix products: 26 us -> 0 us
  between operations: 13.3 us -> 0.01 us
  starting transfers between devices: 9.88 us -> 0 us
  other arithmetic: 9.84 us -> 0 us
  local copies, waits for them, and re-layouts: 7.57 us -> 1.77 us
    all_gather x4 -> x0, waiting for transfers between devices: 167 us -> none  [the longest x1 66.5 us: attention_layer(): gathered = lax.all_gather(block_rows, 'tensor', axis=1, tiled=True)]
    pallas_call x0 -> x1, Pallas kernels: none -> 145 us  [shards(): pl.pallas_call(kernel, out_shape=jax.ShapeDtypeStruct((ROWS, WIDE), BF),...]
    reduce_scatter x1 -> x0, waiting for transfers between devices: 81.9 us -> none  [attention_layer(): lax.psum_scatter(terms.astype(jnp.bfloat16), 'tensor', scatter_dimension=...]
    all_to_all x2 -> x0, waiting for transfers between devices: 17.2 us -> none  [the longest x1 15.5 us: shards(): lax.all_to_all(outgoing, 'dp', split_axis=0, concat_axis=0, tiled=True)]
    dot_general x6 -> x0, matrix products: 16 us -> none  [the longest x1 8.82 us: attention_layer(): jnp.dot(context, lax.all_gather(output_weight, 'dp', axis=1, tiled=True),...]
    reshape x1 -> x0, matrix products: 9.3 us -> none  [attention_layer(): query_accumulated.reshape(row_count, head_count, HD)]
    all_to_all x2 -> x0, starting transfers between devices: 7.94 us -> none  [the longest x1 4.38 us: shards(): lax.all_to_all(slot_flags, 'dp', split_axis=0, concat_axis=0, tiled=True)]
    reduce_sum x2 -> x0, other arithmetic: 4.94 us -> none  [the longest x1 4.1 us: attention_layer(): jnp.mean(widened * widened, axis=1, keepdims=True) + EPSILON]
  transfers between devices with their start and end apart: 8 -> 0, of which waited for: 8 -> 0; matrix products, arithmetic and copies ran while one was open for 8% -> 0% of each run, Pallas kernels for 0% -> 0%
where the time goes in v2:
time: 147 us; the launch traced here: 146 us
  Pallas kernels  145 us (99%)
  local copies, waits for them, and re-layouts  1.77 us (1%)
    pallas_call x1, Pallas kernels, shards(): pl.pallas_call(kernel, out_shape=jax.ShapeDtypeStruct((ROWS, WIDE), BF),...  145 us

profile of v2, /device:TPU:0, one launch (start us, length us, event | category | flops | bytes accessed | tf_op | source)
XLA Modules:
  0.0 146.4 jit_solution(1134699891477418780)
XLA Ops:
  0.0 144.7 %shard_map.91 = bf16[384,512]{1,0:T(8,128)(2,1)} custom-call(s32[16]{0:T(128)} %exited.1, s32[16]{0:T(128)} %destination.1, bf16[16,64,512]{2,1,0:T(8,128)(2,1)} %bitcast.2, f32[16,1,512]{2,1,0:T(1,128)} %bitcast.3, bf16[1024,512]{1,0:T(8,128)(2,1)} %wq.1, bf16[1024,128]{1,0:T(8,128)(2,1)} %wkv.1, bf16[512,1024]{1,0:T(8,128)(2,1)} %wo.1, ...), custom_call_target="tpu_custom_call" | custom-call | flops 7247757312 | bytes 8388608 | tf_op jit(solution)/shard_map/pallas_call | solution.py:501
  144.7 1.8 %copy.11 = bf16[384,512]{1,0:T(8,128)(2,1)} copy(bf16[384,512]{1,0:T(8,128)(2,1)} %shard_map.91) | data formatting | bytes 786432

commit v3 on v2

v3 whole, which is shorter than its diff:
```python
import functools

import jax
import jax.numpy as jnp
import numpy as np
from jax import lax
from jax.experimental import pallas as pl
from jax.experimental.pallas import tpu as pltpu
from jax.sharding import PartitionSpec as P

MESH = pl.DeviceIdType.MESH

HD = 128
ITEM_LEN = 64
HERE = 16
TAKEN = 6
ROWS = TAKEN * ITEM_LEN
WIDE = 512
DEPTH = 1024
EPSILON = 1e-05
THETA = 500000.0
BF = jnp.bfloat16
F32 = jnp.float32

PIECE = DEPTH // 4
HALF = ROWS // 2
QUARTER = ROWS // 4


def tables():
    j = np.arange(HD // 2, dtype=np.float64)
    freq = (THETA ** (-2.0 * j / HD)).astype(np.float32)
    phase = (np.arange(ITEM_LEN, dtype=np.float32)[:, None] * freq).astype(np.float64)
    cos, sin = np.cos(phase), np.sin(phase)
    return (
        np.concatenate([cos, cos], axis=1).astype(np.float32),
        np.concatenate([-sin, sin], axis=1).astype(np.float32),
    )


def kernel(
    exited, destination, hidden, gain_in, wq, wkv, wo, cos_in, sin_in, result,
    gain, cos, sin, out,
    hid, outgoing, arrived, meta, meta_scalar, act, scaled, wbuf, obuf, acc, squares, qs, kvown, kvpart,
    ctx, part, r1, r2, s1, q1, q2,
    local_sem, out_sem, meta_s, meta_r, route_s, route_r, x_s, x_r, ag_s, ag_r, rs_s, rs_r, kv_s, kv_r,
):
    me = lax.axis_index("dp")
    t = lax.axis_index("tensor")
    x, c = me // 2, me % 2
    z, y = t // 4, t % 4
    left = ((x + 3) % 4) * 2 + c
    right = ((x + 1) % 4) * 2 + c
    far = ((x + 2) % 4) * 2 + c
    zp, zm, zf = (z + 1) % 4, (z + 3) % 4, (z + 2) % 4
    yp, ym, yf = (y + 1) % 4, (y + 3) % 4, (y + 2) % 4

    def sibling(i):
        return i + 1 - 2 * c

    sib = sibling(me)

    started = []

    def put(src, dst, send, recv, device):
        copy = pltpu.make_async_remote_copy(
            src_ref=src, dst_ref=dst, send_sem=send, recv_sem=recv,
            device_id=device, device_id_type=MESH,
        )
        copy.start()
        started.append(copy)

    def got(dst, recv):
        pltpu.make_async_remote_copy(
            src_ref=dst, dst_ref=dst, send_sem=recv, recv_sem=recv,
            device_id=(sib, t), device_id_type=MESH,
        ).wait_recv()

    loads = [pltpu.make_async_copy(hidden, hid, local_sem.at[0])]
    loads.append(pltpu.make_async_copy(wq, wbuf.at[me, :, pl.ds(0, WIDE)], local_sem.at[1]))
    loads.append(pltpu.make_async_copy(wkv, wbuf.at[me, :, pl.ds(WIDE, HD)], local_sem.at[2]))
    for s in range(4):
        for h in range(2):
            loads.append(
                pltpu.make_async_copy(
                    wo.at[:, pl.ds(h * WIDE + s * HD, HD)],
                    obuf.at[s, me, :, pl.ds(h * HD, HD)],
                    local_sem.at[3 + 2 * s + h],
                )
            )
    loads.append(pltpu.make_async_copy(gain_in, gain, local_sem.at[12]))
    loads.append(pltpu.make_async_copy(cos_in, cos, local_sem.at[13]))
    loads.append(pltpu.make_async_copy(sin_in, sin, local_sem.at[14]))
    for load in loads:
        load.start()

    barrier = pltpu.get_barrier_semaphore()
    peers = [((me + k) % 8, t) for k in range(1, 8)]
    peers += [(me, zp * 4 + y), (me, zm * 4 + y), (me, z * 4 + yp), (me, z * 4 + ym)]
    for peer in peers:
        pl.semaphore_signal(barrier, inc=1, device_id=peer, device_id_type=MESH)
    pl.semaphore_wait(barrier, len(peers))

    def weights(r, i, low=0, count=None):
        if r < 4:
            return wbuf.at[i, pl.ds(r * PIECE + low, count or PIECE), :]
        return obuf.at[r - 4, i, pl.ds(low, count or WIDE), :]

    def half_of(r):
        return PIECE // 2 if r < 4 else WIDE // 2

    def x_put(r, k, view, device):
        put(view, view, x_s.at[r, k], x_r.at[r, k], (device, t))

    def x_own_sibling(r):
        x_put(r, 6, weights(r, me), sib)

    def x_own(r, which):
        n = half_of(r)
        x_put(r, 2 * which, weights(r, me, which * n, n), right)
        x_put(r, 2 * which + 1, weights(r, me, n - which * n, n), left)

    def x_hand_on(r):
        n = half_of(r)
        got(weights(r, left, 0, n), x_r.at[r, 0])
        x_put(r, 4, weights(r, left, 0, n), right)
        got(weights(r, right, n, n), x_r.at[r, 1])
        x_put(r, 5, weights(r, right, n, n), left)

    def x_near(r, *after):
        n = half_of(r)
        got(weights(r, left, n, n), x_r.at[r, 2])
        got(weights(r, right, 0, n), x_r.at[r, 3])
        for piece in after:
            x_own(*piece)
        x_put(r, 7, weights(r, left), sib)
        x_put(r, 8, weights(r, right), sib)

    def x_far(r, *after):
        n = half_of(r)
        got(weights(r, far, 0, n), x_r.at[r, 4])
        got(weights(r, far, n, n), x_r.at[r, 5])
        for piece in after:
            x_own(*piece)
        x_put(r, 9, weights(r, far, 0, n), sib)
        x_put(r, 10, weights(r, far, n, n), sib)

    def x_sibling(r):
        n = half_of(r)
        got(weights(r, sib), x_r.at[r, 6])
        got(weights(r, sibling(left)), x_r.at[r, 7])
        got(weights(r, sibling(right)), x_r.at[r, 8])
        got(weights(r, sibling(far), 0, n), x_r.at[r, 9])
        got(weights(r, sibling(far), n, n), x_r.at[r, 10])

    loads[1].wait()
    loads[2].wait()
    x_own(0, 0)
    for r in range(4):
        x_own_sibling(r)

    codes = [jnp.where(exited[k] == 0, destination[k], -1) for k in range(HERE)]
    lane = lax.broadcasted_iota(jnp.int32, (8, 128), 1)
    row = jnp.full((8, 128), -1, jnp.int32)
    for k in range(HERE):
        row = jnp.where(lane == k, codes[k], row)
    meta[me] = row
    for k in range(1, 8):
        put(meta.at[me], meta.at[me], meta_s.at[k], meta_r.at[k], ((me + k) % 8, t))

    loads[0].wait()
    for k in [4, 2, 6, 3, 5, 1, 7, 0]:
        dest = (me + k) % 8 if k else me
        seen = jnp.int32(0)
        first = jnp.int32(0)
        second = jnp.int32(0)
        for item in range(HERE):
            hit = codes[item] == dest
            first = jnp.where(hit & (seen == 0), item, first)
            second = jnp.where(hit & (seen == 1), item, second)
            seen = seen + jnp.where(hit, 1, 0)
        if k:
            outgoing[dest, 0] = hid[first]
            outgoing[dest, 1] = hid[second]
            put(outgoing.at[dest], arrived.at[me], route_s.at[k], route_r.at[k], (dest, t))
        else:
            arrived[me, 0] = hid[first]
            arrived[me, 1] = hid[second]
    for load in loads[3:11]:
        load.wait()
    for r in range(4, 8):
        x_own_sibling(r)

    for k in range(1, 8):
        got(meta.at[(me + 8 - k) % 8], meta_r.at[k])
    to_scalar = pltpu.make_async_copy(meta, meta_scalar, local_sem.at[11])
    to_scalar.start()
    to_scalar.wait()
    picks = [jnp.int32(0)] * TAKEN
    rank = jnp.int32(0)
    for j in range(8):
        count = jnp.int32(0)
        for item in range(HERE):
            count = count + jnp.where(meta_scalar[j, 0, item] == me, 1, 0)
        for s in range(2):
            valid = count > s
            for r in range(TAKEN):
                picks[r] = jnp.where(valid & (rank == r), 2 * j + s, picks[r])
            rank = rank + jnp.where(valid, 1, 0)

    for k in range(1, 8):
        got(arrived.at[(me + 8 - k) % 8], route_r.at[k])
    flat = arrived.reshape(16, ITEM_LEN, WIDE)
    for r in range(TAKEN):
        act[t, pl.ds(r * ITEM_LEN, ITEM_LEN), :] = flat[picks[r]]

    def line(half, phase):
        along_z = (half == 0) == (phase == 0)
        if along_z:
            return (z, zm, zp, zf), lambda a, b: a * 4 + b
        return (y, ym, yp, yf), lambda a, b: b * 4 + a

    def chunk(tt, half, low=0, count=HALF):
        return act.at[tt, pl.ds(half * HALF + low, count), :]

    def ag_put(half, k, view, device):
        put(view, view, ag_s.at[half, k], ag_r.at[half, k], (me, device))

    def other(half):
        return y if half == 0 else z

    def ag_send(half, phase, base, tt, near):
        (own, minus, plus, opposite), at = line(half, phase)
        place = other(half) if phase == 0 else near
        ag_put(half, base, chunk(tt, half), at(plus, place))
        ag_put(half, base + 1, chunk(tt, half), at(minus, place))

    def ag_near(half, phase, base, place):
        (own, minus, plus, opposite), at = line(half, phase)
        got(chunk(at(minus, place), half), ag_r.at[half, base])
        q = HALF // 2
        here = other(half) if phase == 0 else (z if half == 0 else y)
        ag_put(half, base + 2, chunk(at(minus, place), half, 0, q), at(plus, here))
        got(chunk(at(plus, place), half), ag_r.at[half, base + 1])
        ag_put(half, base + 3, chunk(at(plus, place), half, q, q), at(minus, here))

    def ag_far(half, phase, base, place):
        (own, minus, plus, opposite), at = line(half, phase)
        q = HALF // 2
        got(chunk(at(opposite, place), half, 0, q), ag_r.at[half, base + 2])
        got(chunk(at(opposite, place), half, q, q), ag_r.at[half, base + 3])

    def places(half):
        return (z, zm, zp, zf) if half == 0 else (y, ym, yp, yf)

    def first_at(half, a):
        return a * 4 + y if half == 0 else z * 4 + a

    def ag2_send(half, n):
        a = places(half)[n]
        ag_send(half, 1, 4 + 4 * n, first_at(half, a), places(half)[0])

    def ag2_near(half, n):
        ag_near(half, 1, 4 + 4 * n, places(half)[n])

    def ag2_far(half, n):
        ag_far(half, 1, 4 + 4 * n, places(half)[n])

    def rotated(value):
        return value * cos[...] + pltpu.roll(value, HD // 2, 1) * sin[...]

    parity = t % 2

    def project(p, low, count):
        @pl.loop(0, 8, step=2)
        def _(i):
            term = None
            for j in range(2):
                product = jnp.dot(
                    scaled[2 * (i + j) + p // 2, :, pl.ds((p % 2) * PIECE, PIECE)],
                    wbuf[i + j, pl.ds(p * PIECE, PIECE), pl.ds(low, count)],
                    preferred_element_type=F32,
                )
                term = product if term is None else term + product
            acc[:, pl.ds(low, count)] += term

    def multiply(s):
        x_sibling(4 + s)

        @pl.loop(0, 4)
        def _(a):
            for b in range(2):
                term = jnp.dot(
                    ctx[...], obuf[s, 2 * a + b], preferred_element_type=F32
                ).astype(BF)
                part[s, a, 2 * b] = term[:, :HD]
                part[s, a, 2 * b + 1] = term[:, HD:]

    def rs_put(s, half, k, src, dst, device):
        put(src, dst, rs_s.at[s, half, k], rs_r.at[s, half, k], (me, device))

    A = (0, QUARTER)
    B = (QUARTER, QUARTER)

    def block(s, half, a, rows):
        low, count = rows
        span = pl.ds(half * HALF + low, count)
        if half == 0:
            return part.at[s, a, :, span, :]
        return part.at[s, :, a, span, :]

    def devices(half, phase):
        if (half == 0) == (phase == 0):
            return zp * 4 + y, zm * 4 + y
        return z * 4 + yp, z * 4 + ym

    def ends(half, phase):
        if (half == 0) == (phase == 0):
            return z, zm, zp, zf
        return y, ym, yp, yf

    def span(rows):
        return pl.ds(rows[0], rows[1])

    def send_first(s):
        for half in range(2):
            own, minus, plus, opposite = ends(half, 0)
            up, down = devices(half, 0)
            rs_put(s, half, 0, block(s, half, opposite, A), r1.at[s, half, 0], up)
            rs_put(s, half, 1, block(s, half, opposite, B), r1.at[s, half, 1], down)
            rs_put(s, half, 2, block(s, half, plus, B), r2.at[s, half, 0, :, span(B), :], up)
            rs_put(s, half, 3, block(s, half, minus, A), r2.at[s, half, 1, :, span(A), :], down)

    def add_first(s, half):
        own, minus, plus, opposite = ends(half, 0)
        up, down = devices(half, 0)
        for side, (a, rows, device) in enumerate(((plus, A, up), (minus, B, down))):
            got(r1.at[s, half, side], rs_r.at[s, half, side])
            view = block(s, half, a, rows)
            view[...] = (view[...].astype(F32) + r1[s, half, side].astype(F32)).astype(BF)
            rs_put(s, half, 4 + side, view, r2.at[s, half, side, :, span(rows), :], device)

    def send_second(s, half):
        own, minus, plus, opposite = ends(half, 0)
        got(r2.at[s, half, 0, :, span(B), :], rs_r.at[s, half, 2])
        got(r2.at[s, half, 1, :, span(A), :], rs_r.at[s, half, 3])
        got(r2.at[s, half, 0, :, span(A), :], rs_r.at[s, half, 4])
        got(r2.at[s, half, 1, :, span(B), :], rs_r.at[s, half, 5])
        view = block(s, half, own, (0, HALF))
        s1[s, half] = (
            view[...].astype(F32) + r2[s, half, 0].astype(F32) + r2[s, half, 1].astype(F32)
        ).astype(BF)
        own, minus, plus, opposite = ends(half, 1)
        up, down = devices(half, 1)
        to = lambda a, rows: s1.at[s, half, a, span(rows), :]
        rs_put(s, half, 6, to(opposite, A), q1.at[s, half, 0], up)
        rs_put(s, half, 7, to(opposite, B), q1.at[s, half, 1], down)
        rs_put(s, half, 8, to(plus, B), q2.at[s, half, 0, span(B), :], up)
        rs_put(s, half, 9, to(minus, A), q2.at[s, half, 1, span(A), :], down)

    def add_second(s, half):
        own, minus, plus, opposite = ends(half, 1)
        up, down = devices(half, 1)
        for side, (a, rows, device) in enumerate(((plus, A, up), (minus, B, down))):
            got(q1.at[s, half, side], rs_r.at[s, half, 6 + side])
            view = s1.at[s, half, a, span(rows), :]
            view[...] = (view[...].astype(F32) + q1[s, half, side].astype(F32)).astype(BF)
            rs_put(s, half, 10 + side, view, q2.at[s, half, side, span(rows), :], device)

    writes = []

    def finish(s, half):
        own, minus, plus, opposite = ends(half, 1)
        got(q2.at[s, half, 0, span(B), :], rs_r.at[s, half, 8])
        got(q2.at[s, half, 1, span(A), :], rs_r.at[s, half, 9])
        got(q2.at[s, half, 0, span(A), :], rs_r.at[s, half, 10])
        got(q2.at[s, half, 1, span(B), :], rs_r.at[s, half, 11])
        rows, cols = pl.ds(half * HALF, HALF), pl.ds(s * HD, HD)
        out[rows, cols] = (
            act[t, rows, cols].astype(F32)
            + s1[s, half, own].astype(F32)
            + q2[s, half, 0].astype(F32)
            + q2[s, half, 1].astype(F32)
        ).astype(BF)
        write = pltpu.make_async_copy(out.at[rows, cols], result.at[rows, cols], out_sem.at[s, half])
        write.start()
        writes.append(write)

    x_own(0, 1)
    ag_send(0, 0, 0, t, None)
    ag_send(1, 0, 0, t, None)
    ag2_send(0, 0)
    ag2_send(1, 0)
    x_hand_on(0)
    x_near(0, (1, 0))
    ag_near(0, 0, 0, other(0))
    ag2_send(0, 1)
    ag2_send(0, 2)
    ag_near(1, 0, 0, other(1))
    ag2_send(1, 1)
    ag2_send(1, 2)
    x_far(0, (1, 1))
    ag2_near(1, 0)
    ag2_near(0, 0)
    x_sibling(0)
    x_hand_on(1)
    ag_far(0, 0, 0, other(0))
    ag2_send(0, 3)
    ag2_near(0, 1)
    x_near(1, (2, 0))
    ag2_near(1, 1)
    ag2_near(0, 2)
    x_far(1, (2, 1))
    ag2_near(1, 2)
    ag_far(1, 0, 0, other(1))
    ag2_send(1, 3)
    x_sibling(1)
    x_hand_on(2)
    ag2_far(1, 0)
    ag2_far(0, 0)
    ag2_far(1, 1)
    x_near(2, (3, 0))
    ag2_far(1, 2)
    ag2_near(0, 3)
    ag2_far(0, 1)
    x_far(2, (3, 1))
    ag2_near(1, 3)
    ag2_far(0, 2)
    x_sibling(2)
    x_hand_on(3)
    ag2_far(0, 3)
    ag2_far(1, 3)
    loads[11].wait()
    acc[...] = jnp.zeros_like(acc)
    squares[...] = jnp.zeros_like(squares)

    @pl.loop(0, 16)
    def _(tt):
        rows = act[tt].astype(F32)
        power = rows * rows
        squares[...] += (power[:, :HD] + power[:, HD:2 * HD]) + (
            power[:, 2 * HD:3 * HD] + power[:, 3 * HD:]
        )
        scaled[tt] = (rows * gain[tt]).astype(BF)

    squares[:, :1] = lax.rsqrt(
        jnp.sum(squares[...], axis=1, keepdims=True) * (1.0 / (16 * WIDE)) + EPSILON
    )
    x_near(3, (4, 0))
    project(0, 0, WIDE + HD)
    project(1, 0, WIDE + HD)
    x_far(3, (4, 1))
    project(2, 0, WIDE + HD)
    x_hand_on(4)
    x_sibling(3)
    project(3, WIDE, HD)
    loads[12].wait()
    loads[13].wait()

    @pl.loop(0, TAKEN, unroll=True)
    def _(n):
        rows = pl.ds(n * ITEM_LEN, ITEM_LEN)
        value = acc[rows, pl.ds(WIDE, HD)] * squares[rows, :1]
        kvown[rows, :] = jnp.where(parity == 0, rotated(value), value).astype(BF)

    put(kvown, kvpart, kv_s, kv_r, (me, t + 1 - 2 * parity))
    project(3, 0, WIDE)

    @pl.loop(0, TAKEN, unroll=True)
    def _(n):
        rows = pl.ds(n * ITEM_LEN, ITEM_LEN)
        inverse = squares[rows, :1]
        for h in range(4):
            value = acc[rows, pl.ds(h * HD, HD)] * inverse
            qs[n, pl.ds(h * ITEM_LEN, ITEM_LEN), :] = rotated(value).astype(BF)

    x_near(4, (5, 0))
    got(kvpart, kv_r)

    @pl.loop(0, TAKEN, unroll=True)
    def _(n):
        rows = pl.ds(n * ITEM_LEN, ITEM_LEN)
        mine, theirs = kvown[rows, :], kvpart[rows, :]
        keys = jnp.where(parity == 0, mine, theirs)
        values = jnp.where(parity == 0, theirs, mine)
        scores = lax.dot_general(
            qs[n], keys, (((1,), (1,)), ((), ())), preferred_element_type=F32
        ) * (HD ** -0.5)
        place = lax.broadcasted_iota(jnp.int32, scores.shape, 0) % ITEM_LEN
        scores = jnp.where(
            place >= lax.broadcasted_iota(jnp.int32, scores.shape, 1), scores, -1e30
        )
        raised = jnp.exp(scores - jnp.max(scores, axis=1, keepdims=True))
        probs = (raised * (1.0 / jnp.sum(raised, axis=1, keepdims=True))).astype(BF)
        context = jnp.dot(probs, values, preferred_element_type=F32).astype(BF)
        for h in range(4):
            ctx[rows, pl.ds(h * HD, HD)] = context[h * ITEM_LEN:(h + 1) * ITEM_LEN, :]

    x_far(4, (5, 1))
    x_hand_on(5)
    multiply(0)
    send_first(0)
    x_near(5, (6, 0))
    x_far(5, (6, 1))
    add_first(0, 0)
    add_first(0, 1)
    multiply(1)
    send_first(1)
    x_hand_on(6)
    send_second(0, 0)
    send_second(0, 1)
    x_near(6, (7, 0))
    add_first(1, 0)
    add_first(1, 1)
    x_far(6, (7, 1))
    add_second(0, 1)
    add_second(0, 0)
    multiply(2)
    send_first(2)
    x_hand_on(7)
    send_second(1, 0)
    send_second(1, 1)
    x_near(7)
    finish(0, 0)
    finish(0, 1)
    add_first(2, 0)
    add_first(2, 1)
    x_far(7)
    add_second(1, 1)
    add_second(1, 0)
    multiply(3)
    send_first(3)
    send_second(2, 0)
    send_second(2, 1)
    finish(1, 0)
    finish(1, 1)
    add_first(3, 0)
    add_first(3, 1)
    add_second(2, 1)
    add_second(2, 0)
    send_second(3, 0)
    send_second(3, 1)
    finish(2, 0)
    finish(2, 1)
    add_second(3, 0)
    add_second(3, 1)
    finish(3, 0)
    finish(3, 1)

    for copy in started:
        copy.wait_send()
    for write in writes:
        write.wait()


def shards(hidden, exited, destination, norm_gain, query_weight, keyvalue_weight, output_weight):
    cos, sin = tables()
    smem = pl.BlockSpec(memory_space=pltpu.SMEM)
    hbm = pl.BlockSpec(memory_space=pl.ANY)
    dma = pltpu.SemaphoreType.DMA
    return pl.pallas_call(
        kernel,
        out_shape=jax.ShapeDtypeStruct((ROWS, WIDE), BF),
        in_specs=[smem, smem, hbm, hbm, hbm, hbm, hbm, hbm, hbm],
        out_specs=hbm,
        scratch_shapes=[
            pltpu.VMEM((16, 1, WIDE), F32),
            pltpu.VMEM((ITEM_LEN, HD), F32),
            pltpu.VMEM((ITEM_LEN, HD), F32),
            pltpu.VMEM((ROWS, WIDE), BF),
            pltpu.VMEM((HERE, ITEM_LEN, WIDE), BF),
            pltpu.VMEM((8, 2, ITEM_LEN, WIDE), BF),
            pltpu.VMEM((8, 2, ITEM_LEN, WIDE), BF),
            pltpu.VMEM((8, 8, 128), jnp.int32),
            pltpu.SMEM((8, 8, 128), jnp.int32),
            pltpu.VMEM((16, ROWS, WIDE), BF),
            pltpu.VMEM((16, ROWS, WIDE), BF),
            pltpu.VMEM((8, DEPTH, WIDE + HD), BF),
            pltpu.VMEM((4, 8, WIDE, 2 * HD), BF),
            pltpu.VMEM((ROWS, WIDE + HD), F32),
            pltpu.VMEM((ROWS, HD), F32),
            pltpu.VMEM((TAKEN, 4 * ITEM_LEN, HD), BF),
            pltpu.VMEM((ROWS, HD), BF),
            pltpu.VMEM((ROWS, HD), BF),
            pltpu.VMEM((ROWS, WIDE), BF),
            pltpu.VMEM((4, 4, 4, ROWS, HD), BF),
            pltpu.VMEM((4, 2, 2, 4, QUARTER, HD), BF),
            pltpu.VMEM((4, 2, 2, 4, HALF, HD), BF),
            pltpu.VMEM((4, 2, 4, HALF, HD), BF),
            pltpu.VMEM((4, 2, 2, QUARTER, HD), BF),
            pltpu.VMEM((4, 2, 2, HALF, HD), BF),
            dma((15,)),
            dma((4, 2)),
            dma((8,)),
            dma((8,)),
            dma((8,)),
            dma((8,)),
            dma((8, 11)),
            dma((8, 11)),
            dma((2, 20)),
            dma((2, 20)),
            dma((4, 2, 12)),
            dma((4, 2, 12)),
            dma(()),
            dma(()),
        ],
        compiler_params=pltpu.CompilerParams(
            collective_id=0, has_side_effects=True, vmem_limit_bytes=60 * 1024 * 1024
        ),
        cost_estimate=pl.CostEstimate(
            flops=2 * ROWS * 16 * WIDE * (2 * WIDE + HD),
            bytes_accessed=8 * 1024 * 1024,
            transcendentals=ROWS * 4 * ITEM_LEN,
        ),
    )(
        exited,
        destination,
        hidden.reshape(HERE, ITEM_LEN, WIDE),
        norm_gain.reshape(16, 1, WIDE),
        query_weight,
        keyvalue_weight,
        output_weight,
        jnp.asarray(cos),
        jnp.asarray(sin),
    )


def solution(mesh):
    placed = (
        P("dp", "tensor"),
        P("dp"),
        P("dp"),
        P(),
        P("dp", "tensor"),
        P("dp", "tensor"),
        P("tensor", "dp"),
    )
    return jax.shard_map(
        shards, mesh=mesh, in_specs=placed, out_specs=P("dp", "tensor"), check_vma=False
    )
```

time: 147 us -> 128 us (0.87)
  Pallas kernels: 145 us -> 126 us
    pallas_call x1, Pallas kernels: 145 us -> 126 us  [shards(): pl.pallas_call(kernel, out_shape=jax.ShapeDtypeStruct((ROWS, WIDE), BF),...]
where the time goes in v3:
time: 128 us
  Pallas kernels  126 us (98%)
  local copies, waits for them, and re-layouts  1.77 us (1%)
    pallas_call x1, Pallas kernels, shards(): pl.pallas_call(kernel, out_shape=jax.ShapeDtypeStruct((ROWS, WIDE), BF),...  126 us

profile of v3, /device:TPU:0, one launch (start us, length us, event | category | flops | bytes accessed | tf_op | source)
XLA Modules:
  0.0 127.9 jit_solution(11042154498728240795)
XLA Ops:
  0.0 126.2 %shard_map.91 = bf16[384,512]{1,0:T(8,128)(2,1)} custom-call(s32[16]{0:T(128)} %exited.1, s32[16]{0:T(128)} %destination.1, bf16[16,64,512]{2,1,0:T(8,128)(2,1)} %bitcast.2, f32[16,1,512]{2,1,0:T(1,128)} %bitcast.3, bf16[1024,512]{1,0:T(8,128)(2,1)} %wq.1, bf16[1024,128]{1,0:T(8,128)(2,1)} %wkv.1, bf16[512,1024]{1,0:T(8,128)(2,1)} %wo.1, ...), custom_call_target="tpu_custom_call" | custom-call | flops 7247757312 | bytes 8388608 | tf_op jit(solution)/shard_map/pallas_call | solution.py:561
  126.2 1.8 %copy.11 = bf16[384,512]{1,0:T(8,128)(2,1)} copy(bf16[384,512]{1,0:T(8,128)(2,1)} %shard_map.91) | data formatting | bytes 786432

commit v4 on v3

--- a/solution.py
+++ b/solution.py
@@ -60,15 +60,12 @@
 
     sib = sibling(me)
 
-    started = []
-
     def put(src, dst, send, recv, device):
         copy = pltpu.make_async_remote_copy(
             src_ref=src, dst_ref=dst, send_sem=send, recv_sem=recv,
             device_id=device, device_id_type=MESH,
         )
         copy.start()
-        started.append(copy)
 
     def got(dst, recv):
         pltpu.make_async_remote_copy(
@@ -76,21 +73,30 @@
             device_id=(sib, t), device_id_type=MESH,
         ).wait_recv()
 
+    def sent(src, send):
+        pltpu.make_async_remote_copy(
+            src_ref=src, dst_ref=src, send_sem=send, recv_sem=send,
+            device_id=(sib, t), device_id_type=MESH,
+        ).wait_send()
+
+    def loaded(dst, sem):
+        pltpu.make_async_copy(dst, dst, sem).wait()
+
     loads = [pltpu.make_async_copy(hidden, hid, local_sem.at[0])]
     loads.append(pltpu.make_async_copy(wq, wbuf.at[me, :, pl.ds(0, WIDE)], local_sem.at[1]))
-    loads.append(pltpu.make_async_copy(wkv, wbuf.at[me, :, pl.ds(WIDE, HD)], local_sem.at[2]))
+    loads.append(pltpu.make_async_copy(wkv, wbuf.at[me, :, pl.ds(WIDE, HD)], local_sem.at[1]))
     for s in range(4):
         for h in range(2):
             loads.append(
                 pltpu.make_async_copy(
                     wo.at[:, pl.ds(h * WIDE + s * HD, HD)],
                     obuf.at[s, me, :, pl.ds(h * HD, HD)],
-                    local_sem.at[3 + 2 * s + h],
+                    local_sem.at[2],
                 )
             )
-    loads.append(pltpu.make_async_copy(gain_in, gain, local_sem.at[12]))
-    loads.append(pltpu.make_async_copy(cos_in, cos, local_sem.at[13]))
-    loads.append(pltpu.make_async_copy(sin_in, sin, local_sem.at[14]))
+    loads.append(pltpu.make_async_copy(gain_in, gain, local_sem.at[3]))
+    loads.append(pltpu.make_async_copy(cos_in, cos, local_sem.at[4]))
+    loads.append(pltpu.make_async_copy(sin_in, sin, local_sem.at[5]))
     for load in loads:
         load.start()
 
@@ -110,51 +116,44 @@
         return PIECE // 2 if r < 4 else WIDE // 2
 
     def x_put(r, k, view, device):
-        put(view, view, x_s.at[r, k], x_r.at[r, k], (device, t))
+        put(view, view, x_s.at[r], x_r.at[r, k], (device, t))
+
+    def shares(r, count):
+        if r < 4:
+            return wbuf.at[pl.ds(0, count), pl.ds(r * PIECE, PIECE), :]
+        return obuf.at[r - 4, pl.ds(0, count)]
 
     def x_own_sibling(r):
-        x_put(r, 6, weights(r, me), sib)
+        x_put(r, 3, weights(r, me), sib)
 
     def x_own(r, which):
         n = half_of(r)
-        x_put(r, 2 * which, weights(r, me, which * n, n), right)
-        x_put(r, 2 * which + 1, weights(r, me, n - which * n, n), left)
+        x_put(r, which, weights(r, me, which * n, n), right)
+        x_put(r, which, weights(r, me, n - which * n, n), left)
 
     def x_hand_on(r):
         n = half_of(r)
-        got(weights(r, left, 0, n), x_r.at[r, 0])
-        x_put(r, 4, weights(r, left, 0, n), right)
-        got(weights(r, right, n, n), x_r.at[r, 1])
-        x_put(r, 5, weights(r, right, n, n), left)
+        got(shares(r, 1), x_r.at[r, 0])
+        x_put(r, 2, weights(r, left, 0, n), right)
+        x_put(r, 2, weights(r, right, n, n), left)
 
     def x_near(r, *after):
-        n = half_of(r)
-        got(weights(r, left, n, n), x_r.at[r, 2])
-        got(weights(r, right, 0, n), x_r.at[r, 3])
+        got(shares(r, 1), x_r.at[r, 1])
         for piece in after:
             x_own(*piece)
-        x_put(r, 7, weights(r, left), sib)
-        x_put(r, 8, weights(r, right), sib)
+        x_put(r, 3, weights(r, left), sib)
+        x_put(r, 3, weights(r, right), sib)
 
     def x_far(r, *after):
-        n = half_of(r)
-        got(weights(r, far, 0, n), x_r.at[r, 4])
-        got(weights(r, far, n, n), x_r.at[r, 5])
+        got(shares(r, 1), x_r.at[r, 2])
         for piece in after:
             x_own(*piece)
-        x_put(r, 9, weights(r, far, 0, n), sib)
-        x_put(r, 10, weights(r, far, n, n), sib)
+        x_put(r, 3, weights(r, far), sib)
 
     def x_sibling(r):
-        n = half_of(r)
-        got(weights(r, sib), x_r.at[r, 6])
-        got(weights(r, sibling(left)), x_r.at[r, 7])
-        got(weights(r, sibling(right)), x_r.at[r, 8])
-        got(weights(r, sibling(far), 0, n), x_r.at[r, 9])
-        got(weights(r, sibling(far), n, n), x_r.at[r, 10])
-
-    loads[1].wait()
-    loads[2].wait()
+        got(shares(r, 4), x_r.at[r, 3])
+
+    loaded(wbuf.at[me], local_sem.at[1])
     x_own(0, 0)
     for r in range(4):
         x_own_sibling(r)
@@ -166,7 +165,7 @@
         row = jnp.where(lane == k, codes[k], row)
     meta[me] = row
     for k in range(1, 8):
-        put(meta.at[me], meta.at[me], meta_s.at[k], meta_r.at[k], ((me + k) % 8, t))
+        put(meta.at[me], meta.at[me], meta_s, meta_r, ((me + k) % 8, t))
 
     loads[0].wait()
     for k in [4, 2, 6, 3, 5, 1, 7, 0]:
@@ -182,18 +181,17 @@
         if k:
             outgoing[dest, 0] = hid[first]
             outgoing[dest, 1] = hid[second]
-            put(outgoing.at[dest], arrived.at[me], route_s.at[k], route_r.at[k], (dest, t))
+            put(outgoing.at[dest], arrived.at[me], route_s, route_r, (dest, t))
         else:
             arrived[me, 0] = hid[first]
             arrived[me, 1] = hid[second]
-    for load in loads[3:11]:
-        load.wait()
+    loaded(obuf.at[pl.ds(0, 4), me], local_sem.at[2])
+    x_own(0, 1)
     for r in range(4, 8):
         x_own_sibling(r)
 
-    for k in range(1, 8):
-        got(meta.at[(me + 8 - k) % 8], meta_r.at[k])
-    to_scalar = pltpu.make_async_copy(meta, meta_scalar, local_sem.at[11])
+    got(meta.at[pl.ds(0, 7)], meta_r)
+    to_scalar = pltpu.make_async_copy(meta, meta_scalar, local_sem.at[6])
     to_scalar.start()
     to_scalar.wait()
     picks = [jnp.int32(0)] * TAKEN
@@ -208,8 +206,7 @@
                 picks[r] = jnp.where(valid & (rank == r), 2 * j + s, picks[r])
             rank = rank + jnp.where(valid, 1, 0)
 
-    for k in range(1, 8):
-        got(arrived.at[(me + 8 - k) % 8], route_r.at[k])
+    got(arrived.at[pl.ds(0, 7)], route_r)
     flat = arrived.reshape(16, ITEM_LEN, WIDE)
     for r in range(TAKEN):
         act[t, pl.ds(r * ITEM_LEN, ITEM_LEN), :] = flat[picks[r]]
@@ -224,31 +221,24 @@
         return act.at[tt, pl.ds(half * HALF + low, count), :]
 
     def ag_put(half, k, view, device):
-        put(view, view, ag_s.at[half, k], ag_r.at[half, k], (me, device))
+        put(view, view, ag_s.at[half], ag_r.at[half, k], (me, device))
 
     def other(half):
         return y if half == 0 else z
 
-    def ag_send(half, phase, base, tt, near):
+    def ag_send(half, phase, slot, tt, near):
         (own, minus, plus, opposite), at = line(half, phase)
         place = other(half) if phase == 0 else near
-        ag_put(half, base, chunk(tt, half), at(plus, place))
-        ag_put(half, base + 1, chunk(tt, half), at(minus, place))
-
-    def ag_near(half, phase, base, place):
+        ag_put(half, slot, chunk(tt, half), at(plus, place))
+        ag_put(half, slot, chunk(tt, half), at(minus, place))
+
+    def ag_near(half, phase, slot, far_slot, place):
         (own, minus, plus, opposite), at = line(half, phase)
-        got(chunk(at(minus, place), half), ag_r.at[half, base])
+        got(act.at[pl.ds(0, 2), pl.ds(half * HALF, HALF), :], ag_r.at[half, slot])
         q = HALF // 2
         here = other(half) if phase == 0 else (z if half == 0 else y)
-        ag_put(half, base + 2, chunk(at(minus, place), half, 0, q), at(plus, here))
-        got(chunk(at(plus, place), half), ag_r.at[half, base + 1])
-        ag_put(half, base + 3, chunk(at(plus, place), half, q, q), at(minus, here))
-
-    def ag_far(half, phase, base, place):
-        (own, minus, plus, opposite), at = line(half, phase)
-        q = HALF // 2
-        got(chunk(at(opposite, place), half, 0, q), ag_r.at[half, base + 2])
-        got(chunk(at(opposite, place), half, q, q), ag_r.at[half, base + 3])
+        ag_put(half, far_slot, chunk(at(minus, place), half, 0, q), at(plus, here))
+        ag_put(half, far_slot, chunk(at(plus, place), half, q, q), at(minus, here))
 
     def places(half):
         return (z, zm, zp, zf) if half == 0 else (y, ym, yp, yf)
@@ -258,13 +248,10 @@
 
     def ag2_send(half, n):
         a = places(half)[n]
-        ag_send(half, 1, 4 + 4 * n, first_at(half, a), places(half)[0])
+        ag_send(half, 1, 2 + n, first_at(half, a), places(half)[0])
 
     def ag2_near(half, n):
-        ag_near(half, 1, 4 + 4 * n, places(half)[n])
-
-    def ag2_far(half, n):
-        ag_far(half, 1, 4 + 4 * n, places(half)[n])
+        ag_near(half, 1, 2 + n, 6, places(half)[n])
 
     def rotated(value):
         return value * cos[...] + pltpu.roll(value, HD // 2, 1) * sin[...]
@@ -272,10 +259,10 @@
     parity = t % 2
 
     def project(p, low, count):
-        @pl.loop(0, 8, step=2)
+        @pl.loop(0, 8, step=8)
         def _(i):
             term = None
-            for j in range(2):
+            for j in range(8):
                 product = jnp.dot(
                     scaled[2 * (i + j) + p // 2, :, pl.ds((p % 2) * PIECE, PIECE)],
                     wbuf[i + j, pl.ds(p * PIECE, PIECE), pl.ds(low, count)],
@@ -287,7 +274,7 @@
     def multiply(s):
         x_sibling(4 + s)
 
-        @pl.loop(0, 4)
+        @pl.loop(0, 4, unroll=True)
         def _(a):
             for b in range(2):
                 term = jnp.dot(
@@ -297,7 +284,7 @@
                 part[s, a, 2 * b + 1] = term[:, HD:]
 
     def rs_put(s, half, k, src, dst, device):
-        put(src, dst, rs_s.at[s, half, k], rs_r.at[s, half, k], (me, device))
+        put(src, dst, rs_s.at[s, half], rs_r.at[s, half, k], (me, device))
 
     A = (0, QUARTER)
     B = (QUARTER, QUARTER)
@@ -327,25 +314,22 @@
             own, minus, plus, opposite = ends(half, 0)
             up, down = devices(half, 0)
             rs_put(s, half, 0, block(s, half, opposite, A), r1.at[s, half, 0], up)
-            rs_put(s, half, 1, block(s, half, opposite, B), r1.at[s, half, 1], down)
-            rs_put(s, half, 2, block(s, half, plus, B), r2.at[s, half, 0, :, span(B), :], up)
-            rs_put(s, half, 3, block(s, half, minus, A), r2.at[s, half, 1, :, span(A), :], down)
+            rs_put(s, half, 0, block(s, half, opposite, B), r1.at[s, half, 1], down)
+            rs_put(s, half, 1, block(s, half, plus, B), r2.at[s, half, 0, :, span(B), :], up)
+            rs_put(s, half, 1, block(s, half, minus, A), r2.at[s, half, 1, :, span(A), :], down)
 
     def add_first(s, half):
         own, minus, plus, opposite = ends(half, 0)
         up, down = devices(half, 0)
+        got(r1.at[s, half], rs_r.at[s, half, 0])
         for side, (a, rows, device) in enumerate(((plus, A, up), (minus, B, down))):
-            got(r1.at[s, half, side], rs_r.at[s, half, side])
             view = block(s, half, a, rows)
             view[...] = (view[...].astype(F32) + r1[s, half, side].astype(F32)).astype(BF)
-            rs_put(s, half, 4 + side, view, r2.at[s, half, side, :, span(rows), :], device)
+            rs_put(s, half, 1, view, r2.at[s, half, side, :, span(rows), :], device)
 
     def send_second(s, half):
         own, minus, plus, opposite = ends(half, 0)
-        got(r2.at[s, half, 0, :, span(B), :], rs_r.at[s, half, 2])
-        got(r2.at[s, half, 1, :, span(A), :], rs_r.at[s, half, 3])
-        got(r2.at[s, half, 0, :, span(A), :], rs_r.at[s, half, 4])
-        got(r2.at[s, half, 1, :, span(B), :], rs_r.at[s, half, 5])
+        got(r2.at[s, half], rs_r.at[s, half, 1])
         view = block(s, half, own, (0, HALF))
         s1[s, half] = (
             view[...].astype(F32) + r2[s, half, 0].astype(F32) + r2[s, half, 1].astype(F32)
@@ -353,28 +337,23 @@
         own, minus, plus, opposite = ends(half, 1)
         up, down = devices(half, 1)
         to = lambda a, rows: s1.at[s, half, a, span(rows), :]
-        rs_put(s, half, 6, to(opposite, A), q1.at[s, half, 0], up)
-        rs_put(s, half, 7, to(opposite, B), q1.at[s, half, 1], down)
-        rs_put(s, half, 8, to(plus, B), q2.at[s, half, 0, span(B), :], up)
-        rs_put(s, half, 9, to(minus, A), q2.at[s, half, 1, span(A), :], down)
+        rs_put(s, half, 2, to(opposite, A), q1.at[s, half, 0], up)
+        rs_put(s, half, 2, to(opposite, B), q1.at[s, half, 1], down)
+        rs_put(s, half, 3, to(plus, B), q2.at[s, half, 0, span(B), :], up)
+        rs_put(s, half, 3, to(minus, A), q2.at[s, half, 1, span(A), :], down)
 
     def add_second(s, half):
         own, minus, plus, opposite = ends(half, 1)
         up, down = devices(half, 1)
+        got(q1.at[s, half], rs_r.at[s, half, 2])
         for side, (a, rows, device) in enumerate(((plus, A, up), (minus, B, down))):
-            got(q1.at[s, half, side], rs_r.at[s, half, 6 + side])
             view = s1.at[s, half, a, span(rows), :]
             view[...] = (view[...].astype(F32) + q1[s, half, side].astype(F32)).astype(BF)
-            rs_put(s, half, 10 + side, view, q2.at[s, half, side, span(rows), :], device)
-
-    writes = []
+            rs_put(s, half, 3, view, q2.at[s, half, side, span(rows), :], device)
 
     def finish(s, half):
         own, minus, plus, opposite = ends(half, 1)
-        got(q2.at[s, half, 0, span(B), :], rs_r.at[s, half, 8])
-        got(q2.at[s, half, 1, span(A), :], rs_r.at[s, half, 9])
-        got(q2.at[s, half, 0, span(A), :], rs_r.at[s, half, 10])
-        got(q2.at[s, half, 1, span(B), :], rs_r.at[s, half, 11])
+        got(q2.at[s, half], rs_r.at[s, half, 3])
         rows, cols = pl.ds(half * HALF, HALF), pl.ds(s * HD, HD)
         out[rows, cols] = (
             act[t, rows, cols].astype(F32)
@@ -382,55 +361,47 @@
             + q2[s, half, 0].astype(F32)
             + q2[s, half, 1].astype(F32)
         ).astype(BF)
-        write = pltpu.make_async_copy(out.at[rows, cols], result.at[rows, cols], out_sem.at[s, half])
-        write.start()
-        writes.append(write)
-
-    x_own(0, 1)
+        pltpu.make_async_copy(out.at[rows, cols], result.at[rows, cols], out_sem).start()
+
     ag_send(0, 0, 0, t, None)
     ag_send(1, 0, 0, t, None)
     ag2_send(0, 0)
     ag2_send(1, 0)
     x_hand_on(0)
     x_near(0, (1, 0))
-    ag_near(0, 0, 0, other(0))
+    ag_near(0, 0, 0, 1, other(0))
     ag2_send(0, 1)
     ag2_send(0, 2)
-    ag_near(1, 0, 0, other(1))
+    x_far(0, (1, 1))
+    ag_near(1, 0, 0, 1, other(1))
     ag2_send(1, 1)
     ag2_send(1, 2)
-    x_far(0, (1, 1))
+    x_sibling(0)
+    x_hand_on(1)
     ag2_near(1, 0)
     ag2_near(0, 0)
-    x_sibling(0)
-    x_hand_on(1)
-    ag_far(0, 0, 0, other(0))
+    got(act.at[0, pl.ds(0 * HALF, HALF), :], ag_r.at[0, 1])
     ag2_send(0, 3)
+    x_near(1, (2, 0))
     ag2_near(0, 1)
-    x_near(1, (2, 0))
     ag2_near(1, 1)
+    x_far(1, (2, 1))
     ag2_near(0, 2)
-    x_far(1, (2, 1))
-    ag2_near(1, 2)
-    ag_far(1, 0, 0, other(1))
-    ag2_send(1, 3)
     x_sibling(1)
     x_hand_on(2)
-    ag2_far(1, 0)
-    ag2_far(0, 0)
-    ag2_far(1, 1)
+    ag2_near(1, 2)
+    got(act.at[0, pl.ds(1 * HALF, HALF), :], ag_r.at[1, 1])
+    ag2_send(1, 3)
     x_near(2, (3, 0))
-    ag2_far(1, 2)
     ag2_near(0, 3)
-    ag2_far(0, 1)
     x_far(2, (3, 1))
-    ag2_near(1, 3)
-    ag2_far(0, 2)
     x_sibling(2)
     x_hand_on(3)
-    ag2_far(0, 3)
-    ag2_far(1, 3)
-    loads[11].wait()
+    ag2_near(1, 3)
+    got(act.at[pl.ds(0, 4), pl.ds(0 * HALF, HALF), :], ag_r.at[0, 6])
+    x_near(3, (4, 0))
+    got(act.at[pl.ds(0, 4), pl.ds(1 * HALF, HALF), :], ag_r.at[1, 6])
+    loaded(gain, local_sem.at[3])
     acc[...] = jnp.zeros_like(acc)
     squares[...] = jnp.zeros_like(squares)
 
@@ -446,16 +417,15 @@
     squares[:, :1] = lax.rsqrt(
         jnp.sum(squares[...], axis=1, keepdims=True) * (1.0 / (16 * WIDE)) + EPSILON
     )
-    x_near(3, (4, 0))
     project(0, 0, WIDE + HD)
+    x_far(3, (4, 1))
     project(1, 0, WIDE + HD)
-    x_far(3, (4, 1))
     project(2, 0, WIDE + HD)
     x_hand_on(4)
     x_sibling(3)
     project(3, WIDE, HD)
-    loads[12].wait()
-    loads[13].wait()
+    loaded(cos, local_sem.at[4])
+    loaded(sin, local_sem.at[5])
 
     @pl.loop(0, TAKEN, unroll=True)
     def _(n):
@@ -463,7 +433,8 @@
         value = acc[rows, pl.ds(WIDE, HD)] * squares[rows, :1]
         kvown[rows, :] = jnp.where(parity == 0, rotated(value), value).astype(BF)
 
-    put(kvown, kvpart, kv_s, kv_r, (me, t + 1 - 2 * parity))
+    put(kvown.at[pl.ds(0 * HALF, HALF), :], kvpart.at[pl.ds(0 * HALF, HALF), :], kv_s, kv_r.at[0], (me, t + 1 - 2 * parity))
+    put(kvown.at[pl.ds(1 * HALF, HALF), :], kvpart.at[pl.ds(1 * HALF, HALF), :], kv_s, kv_r.at[1], (me, t + 1 - 2 * parity))
     project(3, 0, WIDE)
 
     @pl.loop(0, TAKEN, unroll=True)
@@ -475,9 +446,9 @@
             qs[n, pl.ds(h * ITEM_LEN, ITEM_LEN), :] = rotated(value).astype(BF)
 
     x_near(4, (5, 0))
-    got(kvpart, kv_r)
-
-    @pl.loop(0, TAKEN, unroll=True)
+    got(kvpart.at[pl.ds(0 * HALF, HALF), :], kv_r.at[0])
+
+    @pl.loop(0, 3, unroll=True)
     def _(n):
         rows = pl.ds(n * ITEM_LEN, ITEM_LEN)
         mine, theirs = kvown[rows, :], kvpart[rows, :]
@@ -496,14 +467,35 @@
         for h in range(4):
             ctx[rows, pl.ds(h * HD, HD)] = context[h * ITEM_LEN:(h + 1) * ITEM_LEN, :]
 
+    got(kvpart.at[pl.ds(1 * HALF, HALF), :], kv_r.at[1])
+
+    @pl.loop(3, 6, unroll=True)
+    def _(n):
+        rows = pl.ds(n * ITEM_LEN, ITEM_LEN)
+        mine, theirs = kvown[rows, :], kvpart[rows, :]
+        keys = jnp.where(parity == 0, mine, theirs)
+        values = jnp.where(parity == 0, theirs, mine)
+        scores = lax.dot_general(
+            qs[n], keys, (((1,), (1,)), ((), ())), preferred_element_type=F32
+        ) * (HD ** -0.5)
+        place = lax.broadcasted_iota(jnp.int32, scores.shape, 0) % ITEM_LEN
+        scores = jnp.where(
+            place >= lax.broadcasted_iota(jnp.int32, scores.shape, 1), scores, -1e30
+        )
+        raised = jnp.exp(scores - jnp.max(scores, axis=1, keepdims=True))
+        probs = (raised * (1.0 / jnp.sum(raised, axis=1, keepdims=True))).astype(BF)
+        context = jnp.dot(probs, values, preferred_element_type=F32).astype(BF)
+        for h in range(4):
+            ctx[rows, pl.ds(h * HD, HD)] = context[h * ITEM_LEN:(h + 1) * ITEM_LEN, :]
+
     x_far(4, (5, 1))
     x_hand_on(5)
     multiply(0)
     send_first(0)
     x_near(5, (6, 0))
-    x_far(5, (6, 1))
     add_first(0, 0)
     add_first(0, 1)
+    x_far(5, (6, 1))
     multiply(1)
     send_first(1)
     x_hand_on(6)
@@ -520,9 +512,9 @@
     x_hand_on(7)
     send_second(1, 0)
     send_second(1, 1)
-    x_near(7)
     finish(0, 0)
     finish(0, 1)
+    x_near(7)
     add_first(2, 0)
     add_first(2, 1)
     x_far(7)
@@ -540,17 +532,25 @@
     add_second(2, 0)
     send_second(3, 0)
     send_second(3, 1)
+    finish(2, 1)
     finish(2, 0)
-    finish(2, 1)
     add_second(3, 0)
     add_second(3, 1)
     finish(3, 0)
     finish(3, 1)
 
-    for copy in started:
-        copy.wait_send()
-    for write in writes:
-        write.wait()
+    sent(meta.at[pl.ds(0, 7)], meta_s)
+    sent(outgoing.at[pl.ds(0, 7)], route_s)
+    for r in range(8):
+        sent(shares(r, 7), x_s.at[r])
+    for half in range(2):
+        sent(act.at[pl.ds(0, 15), pl.ds(half * HALF, HALF), :], ag_s.at[half])
+    sent(kvown, kv_s)
+    terms = part.reshape(64, ROWS, HD)
+    for s in range(4):
+        for half in range(2):
+            sent(terms.at[pl.ds(16 * s, 15), pl.ds(0, HALF), :], rs_s.at[s, half])
+    loaded(out, out_sem)
 
 
 def shards(hidden, exited, destination, norm_gain, query_weight, keyvalue_weight, output_weight):
@@ -589,20 +589,20 @@
             pltpu.VMEM((4, 2, 4, HALF, HD), BF),
             pltpu.VMEM((4, 2, 2, QUARTER, HD), BF),
             pltpu.VMEM((4, 2, 2, HALF, HD), BF),
-            dma((15,)),
-            dma((4, 2)),
-            dma((8,)),
-            dma((8,)),
-            dma((8,)),
-            dma((8,)),
-            dma((8, 11)),
-            dma((8, 11)),
-            dma((2, 20)),
-            dma((2, 20)),
-            dma((4, 2, 12)),
-            dma((4, 2, 12)),
+            dma((7,)),
             dma(()),
             dma(()),
+            dma(()),
+            dma(()),
+            dma(()),
+            dma((8,)),
+            dma((8, 4)),
+            dma((2,)),
+            dma((2, 7)),
+            dma((4, 2)),
+            dma((4, 2, 4)),
+            dma(()),
+            dma((2,)),
         ],
         compiler_params=pltpu.CompilerParams(
             collective_id=0, has_side_effects=True, vmem_limit_bytes=60 * 1024 * 1024

time: 128 us -> 124 us (0.969)
  Pallas kernels: 126 us -> 122 us
    pallas_call x1, Pallas kernels: 126 us -> 122 us  [shards(): pl.pallas_call(kernel, out_shape=jax.ShapeDtypeStruct((ROWS, WIDE), BF),...]
where the time goes in v4:
time: 124 us; the launch traced here: 123 us
  Pallas kernels  122 us (98%)
  local copies, waits for them, and re-layouts  1.77 us (1%)
    pallas_call x1, Pallas kernels, shards(): pl.pallas_call(kernel, out_shape=jax.ShapeDtypeStruct((ROWS, WIDE), BF),...  122 us

profile of v4, /device:TPU:0, one launch (start us, length us, event | category | flops | bytes accessed | tf_op | source)
XLA Modules:
  0.0 123.5 jit_solution(13269071486428711230)
XLA Ops:
  0.0 121.7 %shard_map.91 = bf16[384,512]{1,0:T(8,128)(2,1)} custom-call(s32[16]{0:T(128)} %exited.1, s32[16]{0:T(128)} %destination.1, bf16[16,64,512]{2,1,0:T(8,128)(2,1)} %bitcast.2, f32[16,1,512]{2,1,0:T(1,128)} %bitcast.3, bf16[1024,512]{1,0:T(8,128)(2,1)} %wq.1, bf16[1024,128]{1,0:T(8,128)(2,1)} %wkv.1, bf16[512,1024]{1,0:T(8,128)(2,1)} %wo.1, ...), custom_call_target="tpu_custom_call" | custom-call | flops 7247757312 | bytes 8388608 | tf_op jit(solution)/shard_map/pallas_call | solution.py:561
  121.7 1.8 %copy.11 = bf16[384,512]{1,0:T(8,128)(2,1)} copy(bf16[384,512]{1,0:T(8,128)(2,1)} %shard_map.91) | data formatting | bytes 786432

commit v5 on v4

--- a/solution.py
+++ b/solution.py
@@ -25,6 +25,7 @@
 PIECE = DEPTH // 4
 HALF = ROWS // 2
 QUARTER = ROWS // 4
+DIRECT = (3,)
 
 
 def tables():
@@ -101,7 +102,8 @@
         load.start()
 
     barrier = pltpu.get_barrier_semaphore()
-    peers = [((me + k) % 8, t) for k in range(1, 8)]
+    peers = [((me + k) % 8, t) for k in (4, 3, 5, 2, 6, 1, 7)]
+    peers += [(me, zf * 4 + y), (me, z * 4 + yf)]
     peers += [(me, zp * 4 + y), (me, zm * 4 + y), (me, z * 4 + yp), (me, z * 4 + ym)]
     for peer in peers:
         pl.semaphore_signal(barrier, inc=1, device_id=peer, device_id_type=MESH)
@@ -148,10 +150,17 @@
         got(shares(r, 1), x_r.at[r, 2])
         for piece in after:
             x_own(*piece)
-        x_put(r, 3, weights(r, far), sib)
+        x_put(r, 4, weights(r, far), sib)
+
+    def x_sibling_near(r):
+        got(shares(r, 3), x_r.at[r, 3])
+
+    def x_sibling_far(r):
+        got(shares(r, 1), x_r.at[r, 4])
 
     def x_sibling(r):
-        got(shares(r, 4), x_r.at[r, 3])
+        x_sibling_near(r)
+        x_sibling_far(r)
 
     loaded(wbuf.at[me], local_sem.at[1])
     x_own(0, 0)
@@ -258,30 +267,29 @@
 
     parity = t % 2
 
-    def project(p, low, count):
-        @pl.loop(0, 8, step=8)
-        def _(i):
-            term = None
-            for j in range(8):
-                product = jnp.dot(
-                    scaled[2 * (i + j) + p // 2, :, pl.ds((p % 2) * PIECE, PIECE)],
-                    wbuf[i + j, pl.ds(p * PIECE, PIECE), pl.ds(low, count)],
-                    preferred_element_type=F32,
-                )
-                term = product if term is None else term + product
-            acc[:, pl.ds(low, count)] += term
-
-    def multiply(s):
-        x_sibling(4 + s)
-
-        @pl.loop(0, 4, unroll=True)
-        def _(a):
+    near_chips, far_chips = [x, (x + 3) % 4, (x + 1) % 4], [(x + 2) % 4]
+    near_shards = [2 * chip + b for chip in near_chips for b in range(2)]
+    far_shards = [2 * chip + b for chip in far_chips for b in range(2)]
+
+    def project(p, low, count, shards):
+        term = None
+        for i in shards:
+            product = jnp.dot(
+                scaled[2 * i + p // 2, :, pl.ds((p % 2) * PIECE, PIECE)],
+                wbuf[i, pl.ds(p * PIECE, PIECE), pl.ds(low, count)],
+                preferred_element_type=F32,
+            )
+            term = product if term is None else term + product
+        acc[:, pl.ds(low, count)] += term
+
+    def multiply(s, chips):
+        for chip in chips:
             for b in range(2):
                 term = jnp.dot(
-                    ctx[...], obuf[s, 2 * a + b], preferred_element_type=F32
+                    ctx[...], obuf[s, 2 * chip + b], preferred_element_type=F32
                 ).astype(BF)
-                part[s, a, 2 * b] = term[:, :HD]
-                part[s, a, 2 * b + 1] = term[:, HD:]
+                part[s, chip, 2 * b] = term[:, :HD]
+                part[s, chip, 2 * b + 1] = term[:, HD:]
 
     def rs_put(s, half, k, src, dst, device):
         put(src, dst, rs_s.at[s, half], rs_r.at[s, half, k], (me, device))
@@ -337,6 +345,13 @@
         own, minus, plus, opposite = ends(half, 1)
         up, down = devices(half, 1)
         to = lambda a, rows: s1.at[s, half, a, span(rows), :]
+        if s in DIRECT:
+            across = zf * 4 + y if half else z * 4 + yf
+            rs_put(s, half, 2, to(opposite, A), q1.at[s, half, 0], across)
+            rs_put(s, half, 2, to(opposite, B), q1.at[s, half, 1], across)
+            rs_put(s, half, 3, to(plus, (0, HALF)), q2.at[s, half, 0], up)
+            rs_put(s, half, 3, to(minus, (0, HALF)), q2.at[s, half, 1], down)
+            return
         rs_put(s, half, 2, to(opposite, A), q1.at[s, half, 0], up)
         rs_put(s, half, 2, to(opposite, B), q1.at[s, half, 1], down)
         rs_put(s, half, 3, to(plus, B), q2.at[s, half, 0, span(B), :], up)
@@ -355,12 +370,16 @@
         own, minus, plus, opposite = ends(half, 1)
         got(q2.at[s, half], rs_r.at[s, half, 3])
         rows, cols = pl.ds(half * HALF, HALF), pl.ds(s * HD, HD)
-        out[rows, cols] = (
+        total = (
             act[t, rows, cols].astype(F32)
             + s1[s, half, own].astype(F32)
             + q2[s, half, 0].astype(F32)
             + q2[s, half, 1].astype(F32)
-        ).astype(BF)
+        )
+        if s in DIRECT:
+            got(q1.at[s, half], rs_r.at[s, half, 2])
+            total = total + q1[s, half].reshape(HALF, HD).astype(F32)
+        out[rows, cols] = total.astype(BF)
         pltpu.make_async_copy(out.at[rows, cols], result.at[rows, cols], out_sem).start()
 
     ag_send(0, 0, 0, t, None)
@@ -369,10 +388,10 @@
     ag2_send(1, 0)
     x_hand_on(0)
     x_near(0, (1, 0))
+    x_far(0, (1, 1))
     ag_near(0, 0, 0, 1, other(0))
     ag2_send(0, 1)
     ag2_send(0, 2)
-    x_far(0, (1, 1))
     ag_near(1, 0, 0, 1, other(1))
     ag2_send(1, 1)
     ag2_send(1, 2)
@@ -384,8 +403,8 @@
     ag2_send(0, 3)
     x_near(1, (2, 0))
     ag2_near(0, 1)
+    x_far(1, (2, 1))
     ag2_near(1, 1)
-    x_far(1, (2, 1))
     ag2_near(0, 2)
     x_sibling(1)
     x_hand_on(2)
@@ -393,8 +412,8 @@
     got(act.at[0, pl.ds(1 * HALF, HALF), :], ag_r.at[1, 1])
     ag2_send(1, 3)
     x_near(2, (3, 0))
+    x_far(2, (3, 1))
     ag2_near(0, 3)
-    x_far(2, (3, 1))
     x_sibling(2)
     x_hand_on(3)
     ag2_near(1, 3)
@@ -417,13 +436,16 @@
     squares[:, :1] = lax.rsqrt(
         jnp.sum(squares[...], axis=1, keepdims=True) * (1.0 / (16 * WIDE)) + EPSILON
     )
-    project(0, 0, WIDE + HD)
     x_far(3, (4, 1))
-    project(1, 0, WIDE + HD)
-    project(2, 0, WIDE + HD)
+    project(0, 0, WIDE + HD, range(8))
+    project(1, 0, WIDE + HD, range(8))
     x_hand_on(4)
-    x_sibling(3)
-    project(3, WIDE, HD)
+    project(2, 0, WIDE + HD, range(8))
+    x_sibling_near(3)
+    project(3, 0, WIDE + HD, near_shards)
+    x_near(4, (5, 0))
+    x_sibling_far(3)
+    project(3, WIDE, HD, far_shards)
     loaded(cos, local_sem.at[4])
     loaded(sin, local_sem.at[5])
 
@@ -435,7 +457,7 @@
 
     put(kvown.at[pl.ds(0 * HALF, HALF), :], kvpart.at[pl.ds(0 * HALF, HALF), :], kv_s, kv_r.at[0], (me, t + 1 - 2 * parity))
     put(kvown.at[pl.ds(1 * HALF, HALF), :], kvpart.at[pl.ds(1 * HALF, HALF), :], kv_s, kv_r.at[1], (me, t + 1 - 2 * parity))
-    project(3, 0, WIDE)
+    project(3, 0, WIDE, far_shards)
 
     @pl.loop(0, TAKEN, unroll=True)
     def _(n):
@@ -445,7 +467,7 @@
             value = acc[rows, pl.ds(h * HD, HD)] * inverse
             qs[n, pl.ds(h * ITEM_LEN, ITEM_LEN), :] = rotated(value).astype(BF)
 
-    x_near(4, (5, 0))
+    x_far(4, (5, 1))
     got(kvpart.at[pl.ds(0 * HALF, HALF), :], kv_r.at[0])
 
     @pl.loop(0, 3, unroll=True)
@@ -488,15 +510,20 @@
         for h in range(4):
             ctx[rows, pl.ds(h * HD, HD)] = context[h * ITEM_LEN:(h + 1) * ITEM_LEN, :]
 
-    x_far(4, (5, 1))
     x_hand_on(5)
-    multiply(0)
+    x_sibling_near(4)
+    multiply(0, near_chips)
+    x_sibling_far(4)
+    multiply(0, far_chips)
     send_first(0)
     x_near(5, (6, 0))
+    x_far(5, (6, 1))
     add_first(0, 0)
     add_first(0, 1)
-    x_far(5, (6, 1))
-    multiply(1)
+    x_sibling_near(5)
+    multiply(1, near_chips)
+    x_sibling_far(5)
+    multiply(1, far_chips)
     send_first(1)
     x_hand_on(6)
     send_second(0, 0)
@@ -505,9 +532,12 @@
     add_first(1, 0)
     add_first(1, 1)
     x_far(6, (7, 1))
+    x_sibling_near(6)
+    multiply(2, near_chips)
     add_second(0, 1)
     add_second(0, 0)
-    multiply(2)
+    x_sibling_far(6)
+    multiply(2, far_chips)
     send_first(2)
     x_hand_on(7)
     send_second(1, 0)
@@ -518,9 +548,12 @@
     add_first(2, 0)
     add_first(2, 1)
     x_far(7)
+    x_sibling_near(7)
+    multiply(3, near_chips)
     add_second(1, 1)
     add_second(1, 0)
-    multiply(3)
+    x_sibling_far(7)
+    multiply(3, far_chips)
     send_first(3)
     send_second(2, 0)
     send_second(2, 1)
@@ -532,10 +565,8 @@
     add_second(2, 0)
     send_second(3, 0)
     send_second(3, 1)
+    finish(2, 0)
     finish(2, 1)
-    finish(2, 0)
-    add_second(3, 0)
-    add_second(3, 1)
     finish(3, 0)
     finish(3, 1)
 
@@ -596,7 +627,7 @@
             dma(()),
             dma(()),
             dma((8,)),
-            dma((8, 4)),
+            dma((8, 5)),
             dma((2,)),
             dma((2, 7)),
             dma((4, 2)),

time: 124 us -> 119 us (0.960)
  Pallas kernels: 122 us -> 117 us
    pallas_call x1, Pallas kernels: 122 us -> 117 us  [shards(): pl.pallas_call(kernel, out_shape=jax.ShapeDtypeStruct((ROWS, WIDE), BF),...]
where the time goes in v5:
time: 119 us
  Pallas kernels  117 us (98%)
  local copies, waits for them, and re-layouts  1.77 us (1%)
    pallas_call x1, Pallas kernels, shards(): pl.pallas_call(kernel, out_shape=jax.ShapeDtypeStruct((ROWS, WIDE), BF),...  117 us

profile of v5, /device:TPU:0, one launch (start us, length us, event | category | flops | bytes accessed | tf_op | source)
XLA Modules:
  0.0 119.1 jit_solution(5848974291772005217)
XLA Ops:
  0.0 117.4 %shard_map.91 = bf16[384,512]{1,0:T(8,128)(2,1)} custom-call(s32[16]{0:T(128)} %exited.1, s32[16]{0:T(128)} %destination.1, bf16[16,64,512]{2,1,0:T(8,128)(2,1)} %bitcast.2, f32[16,1,512]{2,1,0:T(1,128)} %bitcast.3, bf16[1024,512]{1,0:T(8,128)(2,1)} %wq.1, bf16[1024,128]{1,0:T(8,128)(2,1)} %wkv.1, bf16[512,1024]{1,0:T(8,128)(2,1)} %wo.1, ...), custom_call_target="tpu_custom_call" | custom-call | flops 7247757312 | bytes 8388608 | tf_op jit(solution)/shard_map/pallas_call | solution.py:592
  117.4 1.8 %copy.11 = bf16[384,512]{1,0:T(8,128)(2,1)} copy(bf16[384,512]{1,0:T(8,128)(2,1)} %shard_map.91) | data formatting | bytes 786432

commit v6 on v5

--- a/solution.py
+++ b/solution.py
@@ -40,8 +40,8 @@
 
 
 def kernel(
-    exited, destination, hidden, gain_in, wq, wkv, wo, cos_in, sin_in, result,
-    gain, cos, sin, out,
+    exited_in, destination_in, hidden, gain_in, wq, wkv, wo, cos_in, sin_in, result,
+    exited, destination, gain, cos, sin, out,
     hid, outgoing, arrived, meta, meta_scalar, act, scaled, wbuf, obuf, acc, squares, qs, kvown, kvpart,
     ctx, part, r1, r2, s1, q1, q2,
     local_sem, out_sem, meta_s, meta_r, route_s, route_r, x_s, x_r, ag_s, ag_r, rs_s, rs_r, kv_s, kv_r,
@@ -83,6 +83,19 @@
     def loaded(dst, sem):
         pltpu.make_async_copy(dst, dst, sem).wait()
 
+    barrier = pltpu.get_barrier_semaphore()
+    peers = [((me + k) % 8, t) for k in (4, 3, 5, 2, 6, 1, 7)]
+    peers += [(me, zf * 4 + y), (me, z * 4 + yf)]
+    peers += [(me, zp * 4 + y), (me, zm * 4 + y), (me, z * 4 + yp), (me, z * 4 + ym)]
+    for peer in peers:
+        pl.semaphore_signal(barrier, inc=1, device_id=peer, device_id_type=MESH)
+
+    flags = [
+        pltpu.make_async_copy(exited_in, exited, local_sem.at[7]),
+        pltpu.make_async_copy(destination_in, destination, local_sem.at[8]),
+    ]
+    for flag in flags:
+        flag.start()
     loads = [pltpu.make_async_copy(hidden, hid, local_sem.at[0])]
     loads.append(pltpu.make_async_copy(wq, wbuf.at[me, :, pl.ds(0, WIDE)], local_sem.at[1]))
     loads.append(pltpu.make_async_copy(wkv, wbuf.at[me, :, pl.ds(WIDE, HD)], local_sem.at[1]))
@@ -101,14 +114,6 @@
     for load in loads:
         load.start()
 
-    barrier = pltpu.get_barrier_semaphore()
-    peers = [((me + k) % 8, t) for k in (4, 3, 5, 2, 6, 1, 7)]
-    peers += [(me, zf * 4 + y), (me, z * 4 + yf)]
-    peers += [(me, zp * 4 + y), (me, zm * 4 + y), (me, z * 4 + yp), (me, z * 4 + ym)]
-    for peer in peers:
-        pl.semaphore_signal(barrier, inc=1, device_id=peer, device_id_type=MESH)
-    pl.semaphore_wait(barrier, len(peers))
-
     def weights(r, i, low=0, count=None):
         if r < 4:
             return wbuf.at[i, pl.ds(r * PIECE + low, count or PIECE), :]
@@ -162,22 +167,16 @@
         x_sibling_near(r)
         x_sibling_far(r)
 
-    loaded(wbuf.at[me], local_sem.at[1])
-    x_own(0, 0)
-    for r in range(4):
-        x_own_sibling(r)
-
+    for flag in flags:
+        flag.wait()
     codes = [jnp.where(exited[k] == 0, destination[k], -1) for k in range(HERE)]
     lane = lax.broadcasted_iota(jnp.int32, (8, 128), 1)
     row = jnp.full((8, 128), -1, jnp.int32)
     for k in range(HERE):
         row = jnp.where(lane == k, codes[k], row)
     meta[me] = row
-    for k in range(1, 8):
-        put(meta.at[me], meta.at[me], meta_s, meta_r, ((me + k) % 8, t))
-
     loads[0].wait()
-    for k in [4, 2, 6, 3, 5, 1, 7, 0]:
+    for k in range(8):
         dest = (me + k) % 8 if k else me
         seen = jnp.int32(0)
         first = jnp.int32(0)
@@ -190,12 +189,21 @@
         if k:
             outgoing[dest, 0] = hid[first]
             outgoing[dest, 1] = hid[second]
-            put(outgoing.at[dest], arrived.at[me], route_s, route_r, (dest, t))
         else:
             arrived[me, 0] = hid[first]
             arrived[me, 1] = hid[second]
+    loaded(wbuf.at[me], local_sem.at[1])
+    pl.semaphore_wait(barrier, len(peers))
+
+    for k in range(1, 8):
+        put(meta.at[me], meta.at[me], meta_s, meta_r, ((me + k) % 8, t))
+    for k in (4, 2, 6, 3, 5, 1, 7):
+        put(outgoing.at[(me + k) % 8], arrived.at[me], route_s, route_r, ((me + k) % 8, t))
+    x_own(0, 0)
+    x_own(0, 1)
+    for r in range(4):
+        x_own_sibling(r)
     loaded(obuf.at[pl.ds(0, 4), me], local_sem.at[2])
-    x_own(0, 1)
     for r in range(4, 8):
         x_own_sibling(r)
 
@@ -388,37 +396,36 @@
     ag2_send(1, 0)
     x_hand_on(0)
     x_near(0, (1, 0))
-    x_far(0, (1, 1))
     ag_near(0, 0, 0, 1, other(0))
     ag2_send(0, 1)
     ag2_send(0, 2)
     ag_near(1, 0, 0, 1, other(1))
     ag2_send(1, 1)
     ag2_send(1, 2)
-    x_sibling(0)
-    x_hand_on(1)
+    x_far(0, (1, 1))
     ag2_near(1, 0)
     ag2_near(0, 0)
+    x_sibling(0)
     got(act.at[0, pl.ds(0 * HALF, HALF), :], ag_r.at[0, 1])
     ag2_send(0, 3)
+    x_hand_on(1)
+    ag2_near(0, 1)
     x_near(1, (2, 0))
-    ag2_near(0, 1)
-    x_far(1, (2, 1))
     ag2_near(1, 1)
     ag2_near(0, 2)
-    x_sibling(1)
-    x_hand_on(2)
+    x_far(1, (2, 1))
     ag2_near(1, 2)
     got(act.at[0, pl.ds(1 * HALF, HALF), :], ag_r.at[1, 1])
     ag2_send(1, 3)
+    x_sibling(1)
+    x_hand_on(2)
     x_near(2, (3, 0))
+    ag2_near(0, 3)
     x_far(2, (3, 1))
-    ag2_near(0, 3)
+    ag2_near(1, 3)
     x_sibling(2)
+    got(act.at[pl.ds(0, 4), pl.ds(0 * HALF, HALF), :], ag_r.at[0, 6])
     x_hand_on(3)
-    ag2_near(1, 3)
-    got(act.at[pl.ds(0, 4), pl.ds(0 * HALF, HALF), :], ag_r.at[0, 6])
-    x_near(3, (4, 0))
     got(act.at[pl.ds(0, 4), pl.ds(1 * HALF, HALF), :], ag_r.at[1, 6])
     loaded(gain, local_sem.at[3])
     acc[...] = jnp.zeros_like(acc)
@@ -436,14 +443,14 @@
     squares[:, :1] = lax.rsqrt(
         jnp.sum(squares[...], axis=1, keepdims=True) * (1.0 / (16 * WIDE)) + EPSILON
     )
-    x_far(3, (4, 1))
+    x_near(3, (4, 0))
     project(0, 0, WIDE + HD, range(8))
     project(1, 0, WIDE + HD, range(8))
-    x_hand_on(4)
+    x_far(3, (4, 1))
     project(2, 0, WIDE + HD, range(8))
     x_sibling_near(3)
     project(3, 0, WIDE + HD, near_shards)
-    x_near(4, (5, 0))
+    x_hand_on(4)
     x_sibling_far(3)
     project(3, WIDE, HD, far_shards)
     loaded(cos, local_sem.at[4])
@@ -467,7 +474,7 @@
             value = acc[rows, pl.ds(h * HD, HD)] * inverse
             qs[n, pl.ds(h * ITEM_LEN, ITEM_LEN), :] = rotated(value).astype(BF)
 
-    x_far(4, (5, 1))
+    x_near(4, (5, 0))
     got(kvpart.at[pl.ds(0 * HALF, HALF), :], kv_r.at[0])
 
     @pl.loop(0, 3, unroll=True)
@@ -510,16 +517,17 @@
         for h in range(4):
             ctx[rows, pl.ds(h * HD, HD)] = context[h * ITEM_LEN:(h + 1) * ITEM_LEN, :]
 
-    x_hand_on(5)
+    x_far(4, (5, 1))
     x_sibling_near(4)
     multiply(0, near_chips)
     x_sibling_far(4)
     multiply(0, far_chips)
     send_first(0)
+    x_hand_on(5)
     x_near(5, (6, 0))
-    x_far(5, (6, 1))
     add_first(0, 0)
     add_first(0, 1)
+    x_far(5, (6, 1))
     x_sibling_near(5)
     multiply(1, near_chips)
     x_sibling_far(5)
@@ -586,15 +594,16 @@
 
 def shards(hidden, exited, destination, norm_gain, query_weight, keyvalue_weight, output_weight):
     cos, sin = tables()
-    smem = pl.BlockSpec(memory_space=pltpu.SMEM)
     hbm = pl.BlockSpec(memory_space=pl.ANY)
     dma = pltpu.SemaphoreType.DMA
     return pl.pallas_call(
         kernel,
         out_shape=jax.ShapeDtypeStruct((ROWS, WIDE), BF),
-        in_specs=[smem, smem, hbm, hbm, hbm, hbm, hbm, hbm, hbm],
+        in_specs=[hbm, hbm, hbm, hbm, hbm, hbm, hbm, hbm, hbm],
         out_specs=hbm,
         scratch_shapes=[
+            pltpu.SMEM((HERE,), jnp.int32),
+            pltpu.SMEM((HERE,), jnp.int32),
             pltpu.VMEM((16, 1, WIDE), F32),
             pltpu.VMEM((ITEM_LEN, HD), F32),
             pltpu.VMEM((ITEM_LEN, HD), F32),
@@ -620,7 +629,7 @@
             pltpu.VMEM((4, 2, 4, HALF, HD), BF),
             pltpu.VMEM((4, 2, 2, QUARTER, HD), BF),
             pltpu.VMEM((4, 2, 2, HALF, HD), BF),
-            dma((7,)),
+            dma((9,)),
             dma(()),
             dma(()),
             dma(()),

time: 119 us -> 117 us (0.983)
  Pallas kernels: 117 us -> 115 us
    pallas_call x1, Pallas kernels: 117 us -> 115 us  [shards(): pl.pallas_call(kernel, out_shape=jax.ShapeDtypeStruct((ROWS, WIDE), BF),...]
where the time goes in v6:
time: 117 us
  Pallas kernels  115 us (98%)
  local copies, waits for them, and re-layouts  1.77 us (2%)
    pallas_call x1, Pallas kernels, shards(): pl.pallas_call(kernel, out_shape=jax.ShapeDtypeStruct((ROWS, WIDE), BF),...  115 us

profile of v6, /device:TPU:0, one launch (start us, length us, event | category | flops | bytes accessed | tf_op | source)
XLA Modules:
  0.0 116.8 jit_solution(3015874907044254330)
XLA Ops:
  0.0 115.1 %shard_map.91 = bf16[384,512]{1,0:T(8,128)(2,1)} custom-call(s32[16]{0:T(128)} %exited_in.1, s32[16]{0:T(128)} %destination_in.1, bf16[16,64,512]{2,1,0:T(8,128)(2,1)} %bitcast.2, f32[16,1,512]{2,1,0:T(1,128)} %bitcast.3, bf16[1024,512]{1,0:T(8,128)(2,1)} %wq.1, bf16[1024,128]{1,0:T(8,128)(2,1)} %wkv.1, bf16[512,1024]{1,0:T(8,128)(2,1)} %wo.1, ...), custom_call_target="tpu_custom_call" | custom-call | flops 7247757312 | bytes 8388608 | tf_op jit(solution)/shard_map/pallas_call | solution.py:599
  115.1 1.8 %copy.11 = bf16[384,512]{1,0:T(8,128)(2,1)} copy(bf16[384,512]{1,0:T(8,128)(2,1)} %shard_map.91) | data formatting | bytes 786432

commit v7 on v6

--- a/solution.py
+++ b/solution.py
@@ -563,16 +563,16 @@
     x_sibling_far(7)
     multiply(3, far_chips)
     send_first(3)
-    send_second(2, 0)
-    send_second(2, 1)
     finish(1, 0)
     finish(1, 1)
     add_first(3, 0)
     add_first(3, 1)
+    send_second(2, 0)
+    send_second(2, 1)
+    send_second(3, 0)
+    send_second(3, 1)
     add_second(2, 1)
     add_second(2, 0)
-    send_second(3, 0)
-    send_second(3, 1)
     finish(2, 0)
     finish(2, 1)
     finish(3, 0)

time: 117 us -> 117 us (level)
  no operation moved by 1% of the time
where the time goes in v7:
time: 117 us
  Pallas kernels  115 us (98%)
  local copies, waits for them, and re-layouts  1.77 us (2%)
    pallas_call x1, Pallas kernels, shards(): pl.pallas_call(kernel, out_shape=jax.ShapeDtypeStruct((ROWS, WIDE), BF),...  115 us

profile of v7, /device:TPU:0, one launch (start us, length us, event | category | flops | bytes accessed | tf_op | source)
XLA Modules:
  0.0 116.6 jit_solution(7489759044800025899)
XLA Ops:
  0.0 114.8 %shard_map.91 = bf16[384,512]{1,0:T(8,128)(2,1)} custom-call(s32[16]{0:T(128)} %exited_in.1, s32[16]{0:T(128)} %destination_in.1, bf16[16,64,512]{2,1,0:T(8,128)(2,1)} %bitcast.2, f32[16,1,512]{2,1,0:T(1,128)} %bitcast.3, bf16[1024,512]{1,0:T(8,128)(2,1)} %wq.1, bf16[1024,128]{1,0:T(8,128)(2,1)} %wkv.1, bf16[512,1024]{1,0:T(8,128)(2,1)} %wo.1, ...), custom_call_target="tpu_custom_call" | custom-call | flops 7247757312 | bytes 8388608 | tf_op jit(solution)/shard_map/pallas_call | solution.py:599
  114.8 1.8 %copy.11 = bf16[384,512]{1,0:T(8,128)(2,1)} copy(bf16[384,512]{1,0:T(8,128)(2,1)} %shard_map.91) | data formatting | bytes 786432

commit v8 on v7

--- a/solution.py
+++ b/solution.py
@@ -123,7 +123,7 @@
         return PIECE // 2 if r < 4 else WIDE // 2
 
     def x_put(r, k, view, device):
-        put(view, view, x_s.at[r], x_r.at[r, k], (device, t))
+        put(view, view, x_s.at[r // 4], x_r.at[r, k], (device, t))
 
     def shares(r, count):
         if r < 4:
@@ -238,7 +238,7 @@
         return act.at[tt, pl.ds(half * HALF + low, count), :]
 
     def ag_put(half, k, view, device):
-        put(view, view, ag_s.at[half], ag_r.at[half, k], (me, device))
+        put(view, view, ag_s, ag_r.at[half, k], (me, device))
 
     def other(half):
         return y if half == 0 else z
@@ -300,7 +300,7 @@
                 part[s, chip, 2 * b + 1] = term[:, HD:]
 
     def rs_put(s, half, k, src, dst, device):
-        put(src, dst, rs_s.at[s, half], rs_r.at[s, half, k], (me, device))
+        put(src, dst, rs_s, rs_r.at[s, half, k], (me, device))
 
     A = (0, QUARTER)
     B = (QUARTER, QUARTER)
@@ -580,15 +580,11 @@
 
     sent(meta.at[pl.ds(0, 7)], meta_s)
     sent(outgoing.at[pl.ds(0, 7)], route_s)
-    for r in range(8):
-        sent(shares(r, 7), x_s.at[r])
-    for half in range(2):
-        sent(act.at[pl.ds(0, 15), pl.ds(half * HALF, HALF), :], ag_s.at[half])
+    sent(wbuf.at[pl.ds(0, 7)], x_s.at[0])
+    sent(obuf.at[:, pl.ds(0, 7)], x_s.at[1])
+    sent(act.at[pl.ds(0, 15)], ag_s)
     sent(kvown, kv_s)
-    terms = part.reshape(64, ROWS, HD)
-    for s in range(4):
-        for half in range(2):
-            sent(terms.at[pl.ds(16 * s, 15), pl.ds(0, HALF), :], rs_s.at[s, half])
+    sent(part.reshape(64, ROWS, HD).at[pl.ds(0, 60)], rs_s)
     loaded(out, out_sem)
 
 
@@ -635,11 +631,11 @@
             dma(()),
             dma(()),
             dma(()),
-            dma((8,)),
+            dma((2,)),
             dma((8, 5)),
-            dma((2,)),
+            dma(()),
             dma((2, 7)),
-            dma((4, 2)),
+            dma(()),
             dma((4, 2, 4)),
             dma(()),
             dma((2,)),

time: 117 us -> 117 us (level)
  no operation moved by 1% of the time
where the time goes in v8:
time: 117 us; the launch traced here: 116 us
  Pallas kernels  115 us (98%)
  local copies, waits for them, and re-layouts  1.77 us (2%)
    pallas_call x1, Pallas kernels, shards(): pl.pallas_call(kernel, out_shape=jax.ShapeDtypeStruct((ROWS, WIDE), BF),...  115 us

profile of v8, /device:TPU:0, one launch (start us, length us, event | category | flops | bytes accessed | tf_op | source)
XLA Modules:
  0.0 116.5 jit_solution(7060276249758092239)
XLA Ops:
  0.0 114.7 %shard_map.91 = bf16[384,512]{1,0:T(8,128)(2,1)} custom-call(s32[16]{0:T(128)} %exited_in.1, s32[16]{0:T(128)} %destination_in.1, bf16[16,64,512]{2,1,0:T(8,128)(2,1)} %bitcast.2, f32[16,1,512]{2,1,0:T(1,128)} %bitcast.3, bf16[1024,512]{1,0:T(8,128)(2,1)} %wq.1, bf16[1024,128]{1,0:T(8,128)(2,1)} %wkv.1, bf16[512,1024]{1,0:T(8,128)(2,1)} %wo.1, ...), custom_call_target="tpu_custom_call" | custom-call | flops 7247757312 | bytes 8388608 | tf_op jit(solution)/shard_map/pallas_call | solution.py:595
  114.7 1.8 %copy.11 = bf16[384,512]{1,0:T(8,128)(2,1)} copy(bf16[384,512]{1,0:T(8,128)(2,1)} %shard_map.91) | data formatting | bytes 786432

commit v9 on v7

--- a/solution.py
+++ b/solution.py
@@ -331,6 +331,9 @@
             up, down = devices(half, 0)
             rs_put(s, half, 0, block(s, half, opposite, A), r1.at[s, half, 0], up)
             rs_put(s, half, 0, block(s, half, opposite, B), r1.at[s, half, 1], down)
+        for half in range(2):
+            own, minus, plus, opposite = ends(half, 0)
+            up, down = devices(half, 0)
             rs_put(s, half, 1, block(s, half, plus, B), r2.at[s, half, 0, :, span(B), :], up)
             rs_put(s, half, 1, block(s, half, minus, A), r2.at[s, half, 1, :, span(A), :], down)
 

time: 117 us -> 117 us (level)
  no operation moved by 1% of the time
where the time goes in v9:
time: 117 us
  Pallas kernels  115 us (98%)
  local copies, waits for them, and re-layouts  1.77 us (2%)
    pallas_call x1, Pallas kernels, shards(): pl.pallas_call(kernel, out_shape=jax.ShapeDtypeStruct((ROWS, WIDE), BF),...  115 us

profile of v9, /device:TPU:0, one launch (start us, length us, event | category | flops | bytes accessed | tf_op | source)
XLA Modules:
  0.0 116.6 jit_solution(4426335406746830865)
XLA Ops:
  0.0 114.8 %shard_map.91 = bf16[384,512]{1,0:T(8,128)(2,1)} custom-call(s32[16]{0:T(128)} %exited_in.1, s32[16]{0:T(128)} %destination_in.1, bf16[16,64,512]{2,1,0:T(8,128)(2,1)} %bitcast.2, f32[16,1,512]{2,1,0:T(1,128)} %bitcast.3, bf16[1024,512]{1,0:T(8,128)(2,1)} %wq.1, bf16[1024,128]{1,0:T(8,128)(2,1)} %wkv.1, bf16[512,1024]{1,0:T(8,128)(2,1)} %wo.1, ...), custom_call_target="tpu_custom_call" | custom-call | flops 7247757312 | bytes 8388608 | tf_op jit(solution)/shard_map/pallas_call | solution.py:602
  114.8 1.8 %copy.11 = bf16[384,512]{1,0:T(8,128)(2,1)} copy(bf16[384,512]{1,0:T(8,128)(2,1)} %shard_map.91) | data formatting | bytes 786432
